TPU v7x, 512 devices: a whole 4x8x8 slice. The times are simulated.
512 devices in a mesh: rep: 32 (over z, x), tp: 16 (over y, core).
Axes of the slice: x: 4, y: 8, z: 8, core: 2. Of those that a mesh axis runs over, the one named last changes fastest.
Arguments:
- requests: bfloat16 [8192, 16384], P('rep', 'tp'), may hold values from -6 to 6
- value_weight: bfloat16 [16384, 1024], P('tp'), may hold values from -0.0625 to 0.0625
- shrink_weight: bfloat16 [1024, 16, 16384], P('rep', None, 'tp'), may hold values from -0.046875 to 0.046875
- expand_weight: bfloat16 [1024, 16, 1024], P('rep', None, 'tp'), may hold values from -1.5 to 1.5
- destination: int32 [8192], replicated, may hold values from 0 to 31, as said below
- adapter_ids: int32 [8192], replicated, may hold values from 0 to 31
- cache_lists: int32 [32, 32], replicated, may hold values from 0 to 1023, as said below
- home_table: int32 [1024], replicated, may hold values from 0 to 1023, as said below
Outputs:
- adapted: bfloat16 [24576, 1024], P('rep', 'tp')
Inputs may be any that keep to these rules, and one draw needn't show every extreme that they name: `destination`: among the 256 requests of one arrival group at most 24 go to one replica group, and some single replica group receives exactly 24 from every arrival group. `cache_lists`: each row lists 32 distinct adapters, at most 2 of them homed on one replica group (home_table[a] // 32), and exactly 2 on some group in every row. `home_table`: A permutation of the 1024 home positions.
All inputs are finite; a program needn't handle non-finite values.
Results may differ from a plain program's by a relative error of at most 0.001.
Values may be sent and summed in bfloat16 or wider, within the bound.
A program may use at most 64 MiB of HBM per device.

v0:
```python
import jax
import jax.numpy as jnp
from jax import lax
from jax.sharding import PartitionSpec as P

PAIR = 2


def on_device(
    requests,
    value_weight,
    shrink_weight,
    expand_weight,
    destination,
    adapter_ids,
    cache_lists,
    home_table,
):
    groups = lax.axis_size("rep")
    own_group = lax.axis_index("rep")
    tok_dev = requests.shape[0]
    rowcap = 3 * tok_dev // groups
    buffer_rows = groups * rowcap
    home_count = shrink_weight.shape[0]
    cache_len = cache_lists.shape[1]
    rank_width = shrink_weight.shape[1]
    width_out = expand_weight.shape[2]
    places = jnp.arange(cache_len, dtype=jnp.int32)
    blocks = destination.reshape(groups, tok_dev)
    targets = jnp.arange(groups, dtype=jnp.int32)
    member = (blocks[:, :, None] == targets[None, None, :]).astype(jnp.int32)
    earlier = jnp.sum(member * (jnp.cumsum(member, axis=1) - 1), axis=2)
    slot_all = targets[:, None] * rowcap + earlier
    own_slot = lax.dynamic_index_in_dim(
        blocks, own_group, 0, keepdims=False
    ) * rowcap + lax.dynamic_index_in_dim(earlier, own_group, 0, keepdims=False)
    send_rows = (
        jnp.zeros((buffer_rows, requests.shape[1]), requests.dtype).at[own_slot].set(requests)
    )
    arrived = lax.all_to_all(send_rows, "rep", split_axis=0, concat_axis=0, tiled=True)
    landing = jnp.where(blocks == own_group, slot_all, buffer_rows).reshape(-1)
    slot_place = jnp.full((buffer_rows,), -1, jnp.int32).at[landing].set(adapter_ids, mode="drop")
    selector = (slot_place[:, None] == places[None, :]).astype(jnp.float32)
    positions = home_table[cache_lists]
    home_group = positions // home_count
    local_slot = positions % home_count
    homed_here = home_group == own_group
    ranking = jnp.cumsum(homed_here.astype(jnp.int32), axis=1) - 1
    outgoing = jnp.where(homed_here, targets[:, None] * PAIR + ranking, groups * PAIR).reshape(-1)
    send_index = (
        jnp.zeros((groups * PAIR,), jnp.int32).at[outgoing].set(local_slot.reshape(-1), mode="drop")
    )
    send_valid = (
        jnp.zeros((groups * PAIR,), jnp.bfloat16).at[outgoing].set(jnp.bfloat16(1.0), mode="drop")
    )
    send_down = shrink_weight[send_index] * send_valid[:, None, None]
    send_up = expand_weight[send_index] * send_valid[:, None, None]
    got_down, got_up = (
        lax.all_to_all(send_down, "rep", split_axis=0, concat_axis=0, tiled=True),
        lax.all_to_all(send_up, "rep", split_axis=0, concat_axis=0, tiled=True),
    )
    own_homes = lax.dynamic_index_in_dim(home_group, own_group, 0, keepdims=False)
    same_before = jnp.sum(
        ((own_homes[None, :] == own_homes[:, None]) & (places[None, :] < places[:, None])).astype(
            jnp.int32
        ),
        axis=1,
    )
    fetch_index = own_homes * PAIR + same_before
    cached_down = got_down[fetch_index].reshape(cache_len * rank_width, -1)
    cached_up = got_up[fetch_index].reshape(cache_len * rank_width, width_out).astype(jnp.float32)
    shrunk_all = lax.dot_general(
        arrived, cached_down, (((1,), (1,)), ((), ())), preferred_element_type=jnp.float32
    )
    shrunk_part = jnp.sum(
        shrunk_all.reshape(buffer_rows, cache_len, rank_width) * selector[:, :, None], axis=1
    )
    shrunk = lax.psum(shrunk_part, "tp")
    spread_rows = (selector[:, :, None] * shrunk[:, None, :]).reshape(
        buffer_rows, cache_len * rank_width
    )
    expanded = jnp.dot(spread_rows, cached_up, precision=lax.Precision.HIGHEST)
    partial_all = jnp.dot(arrived, value_weight, preferred_element_type=jnp.float32)
    projected = lax.psum_scatter(partial_all, "tp", scatter_dimension=1, tiled=True)
    return (projected + expanded).astype(jnp.bfloat16)


def solution(mesh):
    in_specs = (
        P("rep", "tp"),
        P("tp", None),
        P("rep", None, "tp"),
        P("rep", None, "tp"),
        P(),
        P(),
        P(),
        P(),
    )
    out_specs = P("rep", "tp")
    return jax.shard_map(
        on_device, mesh=mesh, in_specs=in_specs, out_specs=out_specs, check_vma=False
    )
```

profile of v0, /device:TPU:6, one launch (start us, length us, event | category | flops | bytes accessed | tf_op | source)
XLA Modules:
  0.0 252.0 jit_solution(7129162838077101671)
XLA Ops:
  6.5 0.0 copy-start
  6.5 0.9 reshape.239
  7.5 1.9 fusion.14
  9.3 32.3 %reduce-window.6 = s32[32,32,2,128]{3,1,2,0:T(8,128)S(1)} reduce-window(s32[32,32,2,128]{3,1,2,0:T(8,128)} %fusion.14, s32[]{:T(128)} %constant.39.clone.1), window={size=1x1x1x128 pad=0_0x0_0x0_0x127_0}, to_apply=%region_0.0 | reduce-window | flops 33292288 | bytes 2097156 | tf_op jit(solution)/shard_map/reduce-window
  41.7 1.3 slice.18
  43.0 1.7 copy.14
  44.7 0.1 fusion.21
  44.8 0.4 fusion.12
  45.2 3.4 %scatter_custom_fusion = bf16[768,1024]{1,0:T(8,128)(2,1)} fusion(s32[256]{0:T(256)S(1)} %bitcast.56, bf16[256,1024]{1,0:T(8,128)(2,1)} %param.8, bf16[]{:T(256)} %constant.32.clone.1), kind=kCustom, calls=%fused_computation.26 | custom fusion | bytes 1573376 | tf_op jit(solution)/shard_map/scatter | solution.py:38
  48.7 0.0 copy-start.5
  48.7 13.6 %all-to-all-start = ((bf16[32,24,1024]{2,1,0:T(8,128)(2,1)}), bf16[32,24,1024]{2,1,0:T(8,128)(2,1)}, u32[]{:S(2)}, u32[]{:S(2)}) async-start(bf16[32,24,1024]{2,1,0:T(8,128)(2,1)} %bitcast.50), calls=%async_computation | async-start | bytes 3145728 | tf_op jit(solution)/shard_map/all_to_all | solution.py:40
  62.3 0.0 reduce-scatter.2.cloned.1.call-start
  62.3 0.0 copy-done.5
  62.4 0.1 reshape.243
  62.5 0.0 copy-done.1
  62.5 4.5 %gather_fusion = s32[1024]{0:T(1024)S(1)} fusion(s32[1024]{0:T(1024)S(1)} %copy-done.1, s32[1024]{0:T(1024)S(1)} %broadcast_clamp_fusion), kind=kCustom, calls=%fused_computation | custom fusion | bytes 12288 | tf_op jit(solution)/shard_map/gather | solution.py:44
  67.0 0.1 reshape.242
  67.1 34.6 %all-to-all-done = bf16[32,24,1024]{2,1,0:T(8,128)(2,1)} async-done(((bf16[32,24,1024]{2,1,0:T(8,128)(2,1)}), bf16[32,24,1024]{2,1,0:T(8,128)(2,1)}, u32[]{:S(2)}, u32[]{:S(2)}) %all-to-all-start) | async-done | bytes 1572896 | tf_op jit(solution)/shard_map/all_to_all | solution.py:40
  101.7 0.0 copy-done
  101.7 4.9 %fusion.35 = f32[768,1024]{0,1:T(8,128)} fusion(bf16[768,1024]{1,0:T(8,128)(2,1)} %bitcast.6, bf16[1024,1024]{1,0:T(8,128)(2,1)S(1)} %copy-done), kind=kOutput, calls=%fused_computation.77 | convolution fusion | flops 1610612736 | bytes 6815744 | tf_op jit(solution)/shard_map/dot_general | solution.py:83
  106.6 0.0 reduce-scatter.2.cloned.1.call-update
  106.6 0.0 copy-start.2
  106.6 0.2 reduce_window_sum.25
  106.8 0.1 add_add_fusion
  106.9 0.1 add.159
  107.1 4.3 %scatter_custom_fusion.2 = s32[64]{0:T(128)S(1)} fusion(s32[1024]{0:T(1024)S(1)} %bitcast.54, s32[1024]{0:T(1024)S(1)} %add_select_fusion.1, s32[]{:T(128)} %constant.39.clone.1), kind=kCustom, calls=%fused_computation.74 | custom fusion | bytes 260 | tf_op jit(solution)/shard_map/scatter | solution.py:51
  111.4 7.6 %scatter_custom_fusion.3 = bf16[64]{0:T(256)(128)(2,1)S(1)} fusion(s32[1024]{0:T(1024)S(1)} %bitcast.55, bf16[1024]{0:T(1024)(128)(2,1)S(1)} %broadcast.231, bf16[]{:T(256)} %constant.32.clone.1), kind=kCustom, calls=%fused_computation.72 | custom fusion | bytes 130 | tf_op jit(solution)/shard_map/scatter | solution.py:54
  119.0 0.0 copy-done.3
  119.0 1.3 gather_fusion.3
  120.3 1.1 broadcast_multiply_fusion.1
  121.4 0.8 reshape.330
  122.3 5.6 %all-to-all-start.2 = ((bf16[32,2,1024]{2,1,0:T(2,128)(2,1)}), bf16[32,2,1024]{2,1,0:T(2,128)(2,1)S(1)}, u32[]{:S(2)}, u32[]{:S(2)}) async-start(bf16[32,2,1024]{2,1,0:T(2,128)(2,1)} %reshape.330), calls=%async_computation.3 | async-start | bytes 262144 | tf_op jit(solution)/shard_map/all_to_all | solution.py:60
  127.8 0.0 copy-done.2
  127.8 2.0 gather_fusion.1
  129.9 3.2 %broadcast_multiply_fusion = bf16[64,16,1024]{2,1,0:T(8,128)(2,1)} fusion(bf16[64,16,1024]{2,1,0:T(8,128)(2,1)} %gather_fusion.1, bf16[64]{0:T(256)(128)(2,1)S(1)} %scatter_custom_fusion.3), kind=kLoop, calls=%fused_computation.19 | loop fusion | flops 1048576 | bytes 4194432 | tf_op jit(solution)/shard_map/mul | solution.py:56
  133.1 3.7 %all-to-all-done.2 = bf16[32,2,1024]{2,1,0:T(2,128)(2,1)S(1)} async-done(((bf16[32,2,1024]{2,1,0:T(2,128)(2,1)}), bf16[32,2,1024]{2,1,0:T(2,128)(2,1)S(1)}, u32[]{:S(2)}, u32[]{:S(2)}) %all-to-all-start.2) | async-done | bytes 131104 | tf_op jit(solution)/shard_map/all_to_all | solution.py:60
  136.8 6.5 %all-to-all-start.1 = ((bf16[64,16,1024]{2,1,0:T(8,128)(2,1)}), bf16[64,16,1024]{2,1,0:T(8,128)(2,1)}, u32[]{:S(2)}, u32[]{:S(2)}) async-start(bf16[64,16,1024]{2,1,0:T(8,128)(2,1)} %broadcast_multiply_fusion), calls=%async_computation.2 | async-start | bytes 4194304 | tf_op jit(solution)/shard_map/all_to_all | solution.py:59
  143.3 0.1 add_bitcast_fusion.1
  143.4 0.0 copy-done.4
  143.4 30.6 %scatter_custom_fusion.1 = s32[768]{0:T(1024)S(1)} fusion(s32[8192]{0:T(1024)S(1)} %compare_select_fusion, s32[8192]{0:T(1024)} %param.13, s32[]{:T(128)} %constant.45.clone.1), kind=kCustom, calls=%fused_computation.65 | custom fusion | bytes 3584 | tf_op jit(solution)/shard_map/scatter | solution.py:42
  174.1 0.2 convert_reduce_fusion
  174.3 0.2 reshape.331
  174.5 0.6 gather_fusion.4
  175.1 16.0 %all-to-all-done.1 = bf16[64,16,1024]{2,1,0:T(8,128)(2,1)} async-done(((bf16[64,16,1024]{2,1,0:T(8,128)(2,1)}), bf16[64,16,1024]{2,1,0:T(8,128)(2,1)}, u32[]{:S(2)}, u32[]{:S(2)}) %all-to-all-start.1) | async-done | bytes 2097184 | tf_op jit(solution)/shard_map/all_to_all | solution.py:59
  191.2 2.2 gather_fusion.2
  193.4 2.9 %multiply_reduce_fusion = f32[768,16]{0,1:T(8,128)S(1)} fusion(bf16[768,1024,1]{1,0,2:T(8,128)(2,1)} %bitcast.7, bf16[32,16,1024]{2,1,0:T(8,128)(2,1)S(1)} %gather_fusion.2, f32[768,32]{0,1:T(8,128)S(1)} %fusion.20), kind=kOutput, calls=%fused_computation.11 | convolution fusion | flops 806080512 | bytes 2768896 | tf_op jit(solution)/shard_map/dot_general | solution.py:72
  196.3 46.6 %psum.7 = f32[768,16]{0,1:T(8,128)S(1)} all-reduce(f32[768,16]{0,1:T(8,128)S(1)} %multiply_reduce_fusion), channel_id=1, replica_groups=mesh['rep'=32,'tp'=16] {'tp'}, use_global_device_ids=true, to_apply=%region_11.12 | all-reduce | flops 12288 | bytes 98304 | tf_op jit(solution)/shard_map/psum | solution.py:78
  242.8 2.3 fusion.8
  (24 shorter events, 0.2 us)
Async XLA Ops:
  6.5 95.1 %copy-start = (bf16[1024,1024]{1,0:T(8,128)(2,1)S(1)}, bf16[1024,1024]{1,0:T(8,128)(2,1)}, u32[]{:S(2)}) copy-start(bf16[1024,1024]{1,0:T(8,128)(2,1)} %param.9) | copy-start | bytes 6291460
  48.7 13.7 %copy-start.5 = (s32[32,32]{1,0:T(8,128)S(1)}, s32[32,32]{1,0:T(8,128)}, u32[]{:S(2)}) copy-start(s32[32,32]{1,0:T(8,128)} %param.14) | copy-start | bytes 12292
  48.7 13.8 %copy-start.1 = (s32[1024]{0:T(1024)S(1)}, s32[1024]{0:T(1024)}, u32[]{:S(2)}) copy-start(s32[1024]{0:T(1024)} %param.15) | copy-start | bytes 12292
  48.7 53.0 %all-to-all-start = ((bf16[32,24,1024]{2,1,0:T(8,128)(2,1)}), bf16[32,24,1024]{2,1,0:T(8,128)(2,1)}, u32[]{:S(2)}, u32[]{:S(2)}) async-start(bf16[32,24,1024]{2,1,0:T(8,128)(2,1)} %bitcast.50), calls=%async_computation | async-start | bytes 3145728 | tf_op jit(solution)/shard_map/all_to_all | solution.py:40
  62.3 180.5 %reduce-scatter.2.cloned.1.call-start = ((), (), s32[]{:S(2)}) async-start(), calls=%async_computation.4 | async-start | bytes 3342336 | tf_op jit(solution)/shard_map/reduce_scatter | solution.py:84
  106.6 12.4 %copy-start.3 = (bf16[32,16,64]{2,1,0:T(8,128)(2,1)S(1)}, bf16[32,16,64]{2,1,0:T(8,128)(2,1)}, u32[]{:S(2)}) copy-start(bf16[32,16,64]{2,1,0:T(8,128)(2,1)} %param.11) | copy-start | bytes 196612
  106.6 21.2 %copy-start.2 = (bf16[32,16,1024]{2,1,0:T(8,128)(2,1)S(1)}, bf16[32,16,1024]{2,1,0:T(8,128)(2,1)}, u32[]{:S(2)}) copy-start(bf16[32,16,1024]{2,1,0:T(8,128)(2,1)} %param.10) | copy-start | bytes 3145732
  122.3 14.5 %all-to-all-start.2 = ((bf16[32,2,1024]{2,1,0:T(2,128)(2,1)}), bf16[32,2,1024]{2,1,0:T(2,128)(2,1)S(1)}, u32[]{:S(2)}, u32[]{:S(2)}) async-start(bf16[32,2,1024]{2,1,0:T(2,128)(2,1)} %reshape.330), calls=%async_computation.3 | async-start | bytes 262144 | tf_op jit(solution)/shard_map/all_to_all | solution.py:60
  133.1 10.3 %copy-start.4 = (s32[8192]{0:T(1024)S(1)}, s32[8192]{0:T(1024)}, u32[]{:S(2)}) copy-start(s32[8192]{0:T(1024)} %param.12) | copy-start | bytes 98308
  136.8 54.4 %all-to-all-start.1 = ((bf16[64,16,1024]{2,1,0:T(8,128)(2,1)}), bf16[64,16,1024]{2,1,0:T(8,128)(2,1)}, u32[]{:S(2)}, u32[]{:S(2)}) async-start(bf16[64,16,1024]{2,1,0:T(8,128)(2,1)} %broadcast_multiply_fusion), calls=%async_computation.2 | async-start | bytes 4194304 | tf_op jit(solution)/shard_map/all_to_all | solution.py:59
Sparse Core Ops, SparseCore 0:
  106.7 61.1 reduce-scatter.1
where the time goes:
time: 255 us; the launch traced here: 252 us
  local copies, waits for them, and re-layouts  61.9 us (24%)
  waiting for transfers between devices  54.3 us (21%)
  blocking collectives  46.6 us (18%)
  other arithmetic  39.7 us (16%)
  starting transfers between devices  25.7 us (10%)
  between operations  13.7 us (5%)
  matrix products  10.1 us (4%)
    psum x1, blocking collectives, on_device(): shrunk = lax.psum(shrunk_part, 'tp')  46.6 us
    all_to_all x1, waiting for transfers between devices, on_device(): lax.all_to_all(send_rows, 'rep', split_axis=0, concat_axis=0, tiled=True)  34.6 us
    another operation x2, other arithmetic  32.4 us
    scatter x1, local copies, waits for them, and re-layouts, on_device(): jnp.full((buffer_rows,), -1, jnp.int32).at[landing]  30.6 us
    all_to_all x1, waiting for transfers between devices, on_device(): lax.all_to_all(send_down, 'rep', split_axis=0, concat_axis=0, tiled=True)  16 us
    all_to_all x1, starting transfers between devices, on_device(): lax.all_to_all(send_rows, 'rep', split_axis=0, concat_axis=0, tiled=True)  13.6 us
    scatter x1, local copies, waits for them, and re-layouts, on_device(): jnp.zeros((groups * PAIR,), jnp.bfloat16).at[outgoing]  7.58 us
    all_to_all x1, starting transfers between devices, on_device(): lax.all_to_all(send_down, 'rep', split_axis=0, concat_axis=0, tiled=True)  6.49 us
  transfers between devices with their start and end apart: 4, of which 3 were waited for; matrix products, arithmetic and copies ran while one was open for 25% of the time, Pallas kernels for 0%

commit v1 on v0

--- a/solution.py
+++ b/solution.py
@@ -1,12 +1,16 @@
+import functools
+
 import jax
 import jax.numpy as jnp
 from jax import lax
+from jax.experimental import pallas as pl
+from jax.experimental.pallas import tpu as pltpu
 from jax.sharding import PartitionSpec as P
 
 PAIR = 2
 
 
-def on_device(
+def by_serving_group(
     requests,
     value_weight,
     shrink_weight,
@@ -85,6 +89,653 @@
     return (projected + expanded).astype(jnp.bfloat16)
 
 
+MESH = pl.DeviceIdType.MESH
+NX = 4
+ROWS_Z = 64
+ROWS_X = 128
+BACK = 32
+CHUNKS = 4
+LANES = 128
+F32, BF16, I32 = jnp.float32, jnp.bfloat16, jnp.int32
+
+
+def hot(mask):
+    return mask.astype(F32).astype(BF16)
+
+
+def iota(shape, axis):
+    return lax.broadcasted_iota(I32, shape, axis)
+
+
+def nn(a, b):
+    return jnp.dot(a, b, preferred_element_type=F32)
+
+
+def nt(a, b):
+    return lax.dot_general(a, b, (((1,), (1,)), ((), ())), preferred_element_type=F32)
+
+
+def fused_kernel(
+    groups,
+    peers,
+    x_ref,
+    v_ref,
+    a_ref,
+    e_ref,
+    dest_ref,
+    aid_ref,
+    list_ref,
+    table_ref,
+    out_ref,
+    over_ref,
+    send1,
+    recv1,
+    send2,
+    recv2,
+    bsend,
+    brecv,
+    acc,
+    pick2t,
+    pick2,
+    upper,
+    entries,
+    home_s,
+    local_s,
+    slot1_s,
+    slot2_s,
+    mine_s,
+    adp,
+    back_pick,
+    fold,
+    rs_send,
+    rs_recv,
+    ag,
+    xsend,
+    xrecv,
+    osend,
+    send1_sem,
+    recv1_sem,
+    send2_sem,
+    recv2_sem,
+    bsend_sem,
+    brecv_sem,
+    rs_send_sem,
+    rs_recv_sem,
+    ag_send_sem,
+    ag_recv_sem,
+    xsend_sem,
+    xrecv_sem,
+    osend_sem,
+    orecv_sem,
+    local_sem,
+):
+    me = lax.axis_index("rep")
+    mt = lax.axis_index("tp")
+    my = mt // 2
+    mz, mx = me // NX, me % NX
+    nz = groups // NX
+    tok, depth = x_ref.shape
+    part = depth // CHUNKS
+    homes = table_ref.shape[1]
+    cache = list_ref.shape[1] // groups
+    rank = a_ref.shape[0] // homes
+    per = LANES // rank
+    slots = NX * ROWS_X
+    rowcap = out_ref.shape[1]
+
+    barrier = pltpu.get_barrier_semaphore()
+
+    def greet_rep(k, c):
+        pl.semaphore_signal(
+            barrier, inc=1, device_id={"rep": lax.rem(me + k, groups)}, device_id_type=MESH
+        )
+        return c
+
+    def greet_tp(k, c):
+        pl.semaphore_signal(
+            barrier, inc=1, device_id={"tp": lax.rem(mt + k, peers)}, device_id_type=MESH
+        )
+        return c
+
+    lax.fori_loop(1, groups, greet_rep, 0)
+    lax.fori_loop(1, peers, greet_tp, 0)
+
+    upper[...] = hot(iota((tok, tok), 0) < iota((tok, tok), 1))
+
+    listed = list_ref[...]
+    count = groups * cache
+    table = table_ref[...]
+    both = jnp.concatenate([hot_value(table // homes), hot_value(table % homes)], axis=0)
+    major = iota((table.shape[0], count), 0) == listed // homes
+    minor = iota((homes, count), 0) == listed % homes
+    found = nn(both, hot(minor))
+    of_home = jnp.sum(jnp.where(major, found[: table.shape[0]], 0.0), axis=0, keepdims=True)
+    of_local = jnp.sum(jnp.where(major, found[table.shape[0] :], 0.0), axis=0, keepdims=True)
+    owner = iota((groups, count), 1) // cache == iota((groups, count), 0)
+    spread = jnp.concatenate(
+        [jnp.where(owner, of_home, 0.0), jnp.where(owner, of_local, 0.0)], axis=0
+    ).astype(BF16)
+    entries[...] = nn(spread, hot(iota((count, cache), 0) % cache == iota((count, cache), 1))).astype(
+        BF16
+    )
+
+    def look_up(dest, aid):
+        n = dest.shape[1]
+        rows = nn(entries[...], hot(iota((cache, n), 0) == aid))
+        serve = iota((groups, n), 0) == dest
+        home = jnp.sum(jnp.where(serve, rows[:groups], 0.0), axis=0, keepdims=True)
+        local = jnp.sum(jnp.where(serve, rows[groups:], 0.0), axis=0, keepdims=True)
+        return home.astype(I32), local.astype(I32)
+
+    def rank_in(member):
+        earlier = nn(hot(member), upper[...])
+        return jnp.sum(jnp.where(member, earlier, 0.0), axis=0, keepdims=True).astype(I32)
+
+    own_dest = dest_ref[pl.ds(me, 1), :]
+    own_home, _ = look_up(own_dest, aid_ref[pl.ds(me, 1), :])
+    own_plane = own_home // NX
+    own_rank1 = rank_in(iota((nz, tok), 0) == own_plane)
+    own_slot1 = jnp.where(own_rank1 < ROWS_Z, own_plane * ROWS_Z + own_rank1, -1)
+    pick1 = hot(iota((nz * ROWS_Z, tok), 0) == own_slot1)
+
+    def pack(c):
+        rows = nn(pick1, x_ref[:, c * part : (c + 1) * part])
+        send1[c] = rows.astype(BF16).reshape(nz, ROWS_Z, part)
+
+    pack(0)
+    pl.semaphore_wait(barrier, groups + peers - 2)
+
+    def z_step(k):
+        return lax.rem(nz // 2 + (1 - 2 * lax.rem(k, 2)) * ((k + 1) // 2) + nz, nz)
+
+    def z_copy(c, to, frm):
+        return pltpu.make_async_remote_copy(
+            src_ref=send1.at[c, to],
+            dst_ref=recv1.at[c, frm],
+            send_sem=send1_sem.at[c, to],
+            recv_sem=recv1_sem.at[c, frm],
+            device_id={"rep": to * NX + mx},
+            device_id_type=MESH,
+        )
+
+    def x_copy(c, to, frm):
+        return pltpu.make_async_remote_copy(
+            src_ref=send2.at[c, to],
+            dst_ref=recv2.at[c, frm],
+            send_sem=send2_sem.at[c, to],
+            recv_sem=recv2_sem.at[c, frm],
+            device_id={"rep": mz * NX + to},
+            device_id_type=MESH,
+        )
+
+    def z_start(c):
+        def body(k, w):
+            z_copy(c, lax.rem(mz + z_step(k), nz), mz).start()
+            return w
+
+        lax.fori_loop(0, nz - 1, body, 0)
+
+    z_start(0)
+    for c in range(1, CHUNKS):
+        pack(c)
+        z_start(c)
+    for c in range(CHUNKS):
+        recv1[c, mz] = send1[c, mz]
+
+    def target_of(k):
+        z = lax.rem(mz + z_step(k // NX), nz)
+        return z * NX + lax.rem(mx + 1 + lax.rem(k, NX), NX)
+
+    def source_of(k):
+        z = lax.rem(mz + nz - z_step(k // NX), nz)
+        return z * NX + lax.rem(mx + 2 * NX - 1 - lax.rem(k, NX), NX)
+
+    def rep_copy(src, dst, ssem, rsem, to, frm):
+        return pltpu.make_async_remote_copy(
+            src_ref=src.at[to],
+            dst_ref=dst.at[frm],
+            send_sem=ssem.at[to],
+            recv_sem=rsem.at[frm],
+            device_id={"rep": to},
+            device_id_type=MESH,
+        )
+
+    def start_rep(src, dst, ssem, rsem):
+        def body(k, w):
+            rep_copy(src, dst, ssem, rsem, target_of(k), me).start()
+            return w
+
+        lax.fori_loop(0, groups - 1, body, 0)
+
+    def finish_rep_send(src, dst, ssem, rsem):
+        def body(k, w):
+            rep_copy(src, dst, ssem, rsem, target_of(k), me).wait_send()
+            return w
+
+        lax.fori_loop(0, groups - 1, body, 0)
+
+    def finish_rep_recv(src, dst, ssem, rsem):
+        def body(k, w):
+            s = source_of(k)
+            rep_copy(src, dst, ssem, rsem, s, s).wait_recv()
+            return w
+
+        lax.fori_loop(0, groups - 1, body, 0)
+
+    width = bsend.shape[1]
+    step = 256
+    for n in range(v_ref.shape[1] // step):
+        bt = nn(x_ref[...], v_ref[:, n * step : (n + 1) * step]).T
+        for i in range(step // width):
+            bsend[n * (step // width) + i] = bt[i * width : (i + 1) * width]
+
+    def base_copy(to, frm):
+        return pltpu.make_async_remote_copy(
+            src_ref=bsend.at[to],
+            dst_ref=brecv.at[frm],
+            send_sem=bsend_sem.at[to],
+            recv_sem=brecv_sem.at[frm],
+            device_id={"tp": to},
+            device_id_type=MESH,
+        )
+
+    def base_start(k, w):
+        base_copy(lax.rem(mt + k, peers), mt).start()
+        return w
+
+    lax.fori_loop(1, peers, base_start, 0)
+
+    batch = 8
+    counts = jnp.zeros((groups, LANES), F32)
+    for q in range(groups // batch):
+        ids = range(q * batch, (q + 1) * batch)
+        dest = jnp.concatenate([dest_ref[g : g + 1, :] for g in ids], axis=1)
+        aid = jnp.concatenate([aid_ref[g : g + 1, :] for g in ids], axis=1)
+        home, local = look_up(dest, aid)
+        for j, g in enumerate(ids):
+            home_s[g : g + 1, :] = home[:, j * tok : (j + 1) * tok]
+            local_s[g : g + 1, :] = local[:, j * tok : (j + 1) * tok]
+        n = batch * tok
+        counts += nn(
+            hot(iota((groups, n), 0) == home),
+            hot(iota((n, LANES), 0) // tok + q * batch == iota((n, LANES), 1)),
+        )
+    by_plane = nn(hot(iota((nz, groups), 0) == iota((nz, groups), 1) // NX), counts.astype(BF16))
+    by_column = nn(
+        counts.astype(BF16), hot(iota((LANES, LANES), 0) % NX == iota((LANES, LANES), 1))
+    )
+    over = (
+        jnp.max(jnp.where(counts > BACK, 1.0, 0.0), axis=0, keepdims=True)
+        + jnp.max(jnp.where(by_plane > ROWS_Z, 1.0, 0.0), axis=0, keepdims=True)
+        + jnp.max(jnp.where(by_column > ROWS_X, 1.0, 0.0), axis=0, keepdims=True)
+    )
+    over_ref[...] = jnp.broadcast_to(over, over_ref.shape)
+
+    homes_all = home_s[...]
+    before = hot(
+        (iota((groups, groups), 1) % NX == iota((groups, groups), 0) % NX)
+        & (iota((groups, groups), 1) < iota((groups, groups), 0))
+    )
+    ones = jnp.ones((tok, LANES), BF16)
+
+    def rank2(member):
+        picked = hot(member)
+        earlier = nn(picked, upper[...])
+        total = nn(before, nn(picked, ones).astype(BF16))
+        return (earlier + jnp.concatenate([total] * (tok // LANES), axis=1)).astype(I32), earlier
+
+    here = homes_all // NX == mz
+    place1 = nn(hot(here), upper[...]).astype(I32)
+    slot1_s[...] = jnp.where(here & (place1 < ROWS_Z), place1, -1)
+    target = jnp.full((groups, tok), -1, I32)
+    for i in range(NX):
+        member = homes_all == mz * NX + i
+        place, _ = rank2(member)
+        target = jnp.where(member & (place < ROWS_X), i * ROWS_X + place, target)
+    slot2_s[...] = target
+    member = homes_all == me
+    place, back_rank = rank2(member)
+    mine_s[0] = jnp.where(member & (place < ROWS_X), place, -1)
+    mine_s[1] = jnp.where(member, back_rank.astype(I32), -1)
+
+    def route(z, w):
+        g = z * NX + mx
+        first = hot(iota((ROWS_Z, tok), 0) == slot1_s[pl.ds(g, 1), :])
+        second = hot(iota((slots, tok), 0) == slot2_s[pl.ds(g, 1), :])
+        pick2t[pl.ds(pl.multiple_of(z * ROWS_Z, ROWS_Z), ROWS_Z), :] = nt(first, second)
+        return w
+
+    lax.fori_loop(0, nz, route, 0)
+    pick2[...] = pick2t[...].T.astype(BF16)
+
+    adp[...] = jnp.zeros_like(adp)
+    acc[...] = jnp.zeros_like(acc)
+
+    def shrink(c):
+        def wait_x(k, w):
+            frm = lax.rem(mx + k, NX)
+            x_copy(c, frm, frm).wait_recv()
+            return w
+
+        lax.fori_loop(1, NX, wait_x, 0)
+        rows = recv2[c].reshape(slots, part)
+        acc[...] += nt(rows, a_ref[:, c * part : (c + 1) * part])
+
+    def stage(c):
+        def wait_z(k, w):
+            frm = lax.rem(mz + nz - z_step(k), nz)
+            z_copy(c, frm, frm).wait_recv()
+            return w
+
+        lax.fori_loop(0, nz - 1, wait_z, 0)
+        rows = nn(pick2[...], recv1[c].reshape(nz * ROWS_Z, part))
+        send2[c] = rows.astype(BF16).reshape(NX, ROWS_X, part)
+
+        def send_x(k, w):
+            x_copy(c, lax.rem(mx + k, NX), mx).start()
+            return w
+
+        lax.fori_loop(1, NX, send_x, 0)
+        recv2[c, mx] = send2[c, mx]
+
+    def homed(g, w):
+        column = lax.rem(g, NX)
+        second = hot(iota((ROWS_X, tok), 0) == mine_s[0, pl.ds(g, 1), :])
+        back = hot(iota((BACK, tok), 0) == mine_s[1, pl.ds(g, 1), :])
+        value = (local_s[pl.ds(g, 1), :] + 1).astype(F32).astype(BF16)
+        at = pl.ds(pl.multiple_of(column * ROWS_X, ROWS_X), ROWS_X)
+        adp[at, :] += nt(second, jnp.broadcast_to(value, (LANES, tok)))
+        back_pick[column, g // NX] = nt(back, second)
+        return w
+
+    quarter = groups // CHUNKS
+    for c in range(CHUNKS):
+        stage(c)
+        lax.fori_loop(c * quarter, (c + 1) * quarter, homed, 0)
+        if c:
+            shrink(c - 1)
+    column = jnp.broadcast_to(own_home.astype(F32), (LANES, tok))
+    own_back = rank_in(iota((groups, tok), 0) == own_home)
+    own_back = jnp.where(own_back < BACK, own_home * BACK + own_back, -1)
+    column = jnp.broadcast_to(own_back.astype(F32), (LANES, tok)).T[:, 0:1].astype(I32)
+    unpack = hot(iota((tok, groups * BACK), 1) == column)
+    own_out = own_dest * rowcap + rank_in(iota((groups, tok), 0) == own_dest)
+    place_out = hot(iota((groups * rowcap, tok), 0) == own_out)
+    shrink(CHUNKS - 1)
+
+    wanted = adp[...].astype(I32) - 1
+    lane = iota((slots, LANES), 1) // rank
+    folded = jnp.zeros((slots, LANES), F32)
+    for n in range(homes // per):
+        folded += jnp.where(wanted == n * per + lane, acc[:, n * LANES : (n + 1) * LANES], 0.0)
+
+    low = jnp.sum(folded.T.reshape(per, rank, slots), axis=0)
+    tiles = peers // 2
+    half = rank // 2
+    for t in range(tiles):
+        rs_send[t] = low[
+            half * (t % 2) : half * (t % 2 + 1), (t // 2) * LANES : (t // 2 + 1) * LANES
+        ]
+
+    def rs_copy(tile, frm):
+        return pltpu.make_async_remote_copy(
+            src_ref=rs_send.at[tile],
+            dst_ref=rs_recv.at[frm],
+            send_sem=rs_send_sem.at[tile],
+            recv_sem=rs_recv_sem.at[frm],
+            device_id={"tp": 2 * tile},
+            device_id_type=MESH,
+        )
+
+    def ag_copy(tile, to):
+        return pltpu.make_async_remote_copy(
+            src_ref=ag.at[tile],
+            dst_ref=ag.at[tile],
+            send_sem=ag_send_sem.at[to],
+            recv_sem=ag_recv_sem.at[tile],
+            device_id={"tp": to},
+            device_id_type=MESH,
+        )
+
+    def rs_start(k, w):
+        tile = lax.rem(my + tiles // 2 + k, tiles)
+
+        @pl.when(2 * tile != mt)
+        def _():
+            rs_copy(tile, mt).start()
+
+        return w
+
+    lax.fori_loop(0, tiles, rs_start, 0)
+
+    @pl.when(lax.rem(mt, 2) == 0)
+    def _():
+        rs_recv[mt] = rs_send[my]
+
+        def rs_wait(k, w):
+            rs_copy(my, lax.rem(mt + k, peers)).wait_recv()
+            return w
+
+        lax.fori_loop(1, peers, rs_wait, 0)
+        ag[my] = jnp.sum(rs_recv[...], axis=0)
+
+        def ag_start(k, w):
+            ag_copy(my, lax.rem(mt + k, peers)).start()
+            return w
+
+        lax.fori_loop(1, peers, ag_start, 0)
+
+    def ag_wait(k, w):
+        tile = lax.rem(my + k, tiles)
+
+        @pl.when(2 * tile != mt)
+        def _():
+            ag_copy(tile, mt).wait_recv()
+
+        return w
+
+    lax.fori_loop(0, tiles, ag_wait, 0)
+
+    e2 = jnp.concatenate([e_ref[...], e_ref[...]], axis=1)
+    lane1 = iota((ROWS_X, LANES), 1)
+    for y in range(NX):
+        tile = jnp.concatenate([ag[2 * y], ag[2 * y + 1]] * per, axis=0).T
+        chosen = wanted[y * ROWS_X : (y + 1) * ROWS_X]
+        spread = jnp.concatenate(
+            [
+                jnp.where(chosen == n * per + lane1 // rank, tile, 0.0)
+                for n in range(homes // per)
+            ],
+            axis=1,
+        )
+        hi = spread.astype(BF16)
+        lo = (spread - hi.astype(F32)).astype(BF16)
+        full = nn(hi, e2) + nn(lo, e2)
+        top = full.astype(BF16).astype(F32)
+        pair = jnp.where(lane1 < width, full, full - top).astype(BF16)
+        sel = back_pick[y].reshape(nz * BACK, LANES).astype(BF16)
+        rows = nn(sel, pair)
+        for z in range(nz):
+            xsend[z * NX + y] = rows[z * BACK : (z + 1) * BACK].astype(BF16)
+    start_rep(xsend, xrecv, xsend_sem, xrecv_sem)
+    keep2 = pltpu.make_async_copy(xsend.at[me], xrecv.at[me], local_sem.at[0])
+    keep2.start()
+
+    def base_wait(k, w):
+        frm = lax.rem(mt + k, peers)
+        base_copy(frm, frm).wait_recv()
+        return w
+
+    lax.fori_loop(1, peers, base_wait, 0)
+    brecv[mt] = bsend[mt]
+    base = jnp.sum(brecv[...], axis=0)
+
+    keep2.wait()
+    finish_rep_recv(xsend, xrecv, xsend_sem, xrecv_sem)
+    extra = nn(unpack, xrecv[...].reshape(groups * BACK, LANES)).T
+    total = (base + extra[:width] + extra[width:]).astype(BF16)
+    final = nt(place_out, total)
+    for s in range(groups):
+        osend[s] = final[s * rowcap : (s + 1) * rowcap].astype(BF16)
+    start_rep(osend, out_ref, osend_sem, orecv_sem)
+    keep3 = pltpu.make_async_copy(osend.at[me], out_ref.at[me], local_sem.at[1])
+    keep3.start()
+
+    for c in range(CHUNKS):
+
+        def z_sent(k, w):
+            z_copy(c, lax.rem(mz + z_step(k), nz), mz).wait_send()
+            return w
+
+        def x_sent(k, w):
+            x_copy(c, lax.rem(mx + k, NX), mx).wait_send()
+            return w
+
+        lax.fori_loop(0, nz - 1, z_sent, 0)
+        lax.fori_loop(1, NX, x_sent, 0)
+
+    def base_sent(k, w):
+        base_copy(lax.rem(mt + k, peers), mt).wait_send()
+        return w
+
+    lax.fori_loop(1, peers, base_sent, 0)
+
+    def rs_sent(k, w):
+        tile = lax.rem(my + k, tiles)
+
+        @pl.when(2 * tile != mt)
+        def _():
+            rs_copy(tile, mt).wait_send()
+
+        return w
+
+    lax.fori_loop(0, tiles, rs_sent, 0)
+
+    @pl.when(lax.rem(mt, 2) == 0)
+    def _():
+        def ag_sent(k, w):
+            ag_copy(my, lax.rem(mt + k, peers)).wait_send()
+            return w
+
+        lax.fori_loop(1, peers, ag_sent, 0)
+
+    finish_rep_send(xsend, xrecv, xsend_sem, xrecv_sem)
+    keep3.wait()
+    finish_rep_send(osend, out_ref, osend_sem, orecv_sem)
+    finish_rep_recv(osend, out_ref, osend_sem, orecv_sem)
+
+
+def hot_value(a):
+    return a.astype(F32).astype(BF16)
+
+
+def fused(groups, peers, requests, value_weight, shrink, expand, dest, aid, lists, table):
+    tok, depth = requests.shape
+    width = expand.shape[1]
+    rowcap = 3 * tok // groups
+    nz, part, slots = groups // NX, depth // CHUNKS, NX * ROWS_X
+    vmem = pl.BlockSpec(memory_space=pltpu.VMEM)
+    dma = pltpu.SemaphoreType.DMA
+    return pl.pallas_call(
+        functools.partial(fused_kernel, groups, peers),
+        out_shape=[
+            jax.ShapeDtypeStruct((groups, rowcap, width), BF16),
+            jax.ShapeDtypeStruct((8, LANES), F32),
+        ],
+        in_specs=[vmem] * 8,
+        out_specs=[vmem, vmem],
+        scratch_shapes=[
+            pltpu.VMEM((CHUNKS, nz, ROWS_Z, part), BF16),
+            pltpu.VMEM((CHUNKS, nz, ROWS_Z, part), BF16),
+            pltpu.VMEM((CHUNKS, NX, ROWS_X, part), BF16),
+            pltpu.VMEM((CHUNKS, NX, ROWS_X, part), BF16),
+            pltpu.VMEM((peers, width, tok), F32),
+            pltpu.VMEM((peers, width, tok), F32),
+            pltpu.VMEM((slots, shrink.shape[0]), F32),
+            pltpu.VMEM((nz * ROWS_Z, slots), F32),
+            pltpu.VMEM((slots, nz * ROWS_Z), BF16),
+            pltpu.VMEM((tok, tok), BF16),
+            pltpu.VMEM((2 * groups, lists.shape[1] // groups), BF16),
+            pltpu.VMEM((groups, tok), I32),
+            pltpu.VMEM((groups, tok), I32),
+            pltpu.VMEM((groups, tok), I32),
+            pltpu.VMEM((groups, tok), I32),
+            pltpu.VMEM((2, groups, tok), I32),
+            pltpu.VMEM((slots, LANES), F32),
+            pltpu.VMEM((NX, nz, BACK, LANES), F32),
+            pltpu.VMEM((slots, LANES), F32),
+            pltpu.VMEM((peers // 2, 8, LANES), F32),
+            pltpu.VMEM((peers, 8, LANES), F32),
+            pltpu.VMEM((peers // 2, 8, LANES), F32),
+            pltpu.VMEM((groups, BACK, LANES), BF16),
+            pltpu.VMEM((groups, BACK, LANES), BF16),
+            pltpu.VMEM((groups, rowcap, width), BF16),
+            dma((CHUNKS, nz)),
+            dma((CHUNKS, nz)),
+            dma((CHUNKS, NX)),
+            dma((CHUNKS, NX)),
+            dma((peers,)),
+            dma((peers,)),
+            dma((peers // 2,)),
+            dma((peers,)),
+            dma((peers,)),
+            dma((peers // 2,)),
+            dma((groups,)),
+            dma((groups,)),
+            dma((groups,)),
+            dma((groups,)),
+            dma((2,)),
+        ],
+        compiler_params=pltpu.CompilerParams(
+            collective_id=0, has_side_effects=True, vmem_limit_bytes=48 * 1024 * 1024
+        ),
+        name="fused",
+    )(requests, value_weight, shrink, expand, dest, aid, lists, table)
+
+
+def on_device(
+    requests,
+    value_weight,
+    shrink_weight,
+    expand_weight,
+    destination,
+    adapter_ids,
+    cache_lists,
+    home_table,
+):
+    groups = lax.axis_size("rep")
+    tok = requests.shape[0]
+    home_count, rank, depth = shrink_weight.shape
+    width = expand_weight.shape[2]
+    out, over = fused(
+        groups,
+        lax.axis_size("tp"),
+        requests,
+        value_weight,
+        shrink_weight.reshape(home_count * rank, depth),
+        expand_weight.reshape(home_count * rank, width),
+        destination.reshape(groups, tok),
+        adapter_ids.reshape(groups, tok),
+        cache_lists.reshape(1, -1),
+        home_table.reshape(-1, home_count),
+    )
+    out = out.reshape(-1, width)
+
+    def any_input(out):
+        return by_serving_group(
+            requests,
+            value_weight,
+            shrink_weight,
+            expand_weight,
+            destination,
+            adapter_ids,
+            cache_lists,
+            home_table,
+        )
+
+    return lax.cond(jnp.max(over) > 0.0, any_input, lambda out: out, out)
+
+
 def solution(mesh):
     in_specs = (
         P("rep", "tp"),

time: 255 us -> 97.8 us (0.38)
  Pallas kernels: 0 us -> 77.4 us
  local copies, waits for them, and re-layouts: 61.9 us -> 3.88 us
  waiting for transfers between devices: 54.3 us -> 0 us
  blocking collectives: 46.6 us -> 0 us
  other arithmetic: 39.7 us -> 0.6 us
  starting transfers between devices: 25.7 us -> 0 us
  matrix products: 10.1 us -> 0 us
    pallas_call x0 -> x1, Pallas kernels: none -> 77.4 us  [fused(): pl.pallas_call(functools.partial(fused_kernel, groups, peers), out_shape=...]
    all_to_all x3 -> x0, waiting for transfers between devices: 54.3 us -> none  [the longest x1 34.6 us: on_device(): lax.all_to_all(send_rows, 'rep', split_axis=0, concat_axis=0, tiled=True)]
    psum x1 -> x0, blocking collectives: 46.6 us -> none  [on_device(): shrunk = lax.psum(shrunk_part, 'tp')]
    scatter x4 -> x0, local copies, waits for them, and re-layouts: 46 us -> none  [the longest x1 30.6 us: on_device(): jnp.full((buffer_rows,), -1, jnp.int32).at[landing]]
    another operation x3 -> x0, other arithmetic: 32.6 us -> none
    all_to_all x3 -> x0, starting transfers between devices: 25.7 us -> none  [the longest x1 13.6 us: on_device(): lax.all_to_all(send_rows, 'rep', split_axis=0, concat_axis=0, tiled=True)]
    gather x6 -> x0, local copies, waits for them, and re-layouts: 10.8 us -> none  [the longest x2 4.59 us: on_device(): positions = home_table[cache_lists]]
    dot_general x3 -> x0, matrix products: 10.1 us -> none  [the longest x1 4.92 us: on_device(): jnp.dot(arrived, value_weight, preferred_element_type=jnp.float32)]
  transfers between devices with their start and end apart: 4 -> 0, of which waited for: 3 -> 0; matrix products, arithmetic and copies ran while one was open for 25% -> 0% of each run, Pallas kernels for 0% -> 0%
where the time goes in v1:
time: 97.8 us; the launch traced here: 96.3 us
  Pallas kernels  77.4 us (79%)
  between operations  14.1 us (14%)
  local copies, waits for them, and re-layouts  3.88 us (4%)
    pallas_call x1, Pallas kernels, fused(): pl.pallas_call(functools.partial(fused_kernel, groups, peers), out_shape=...  77.4 us

profile of v1, /device:TPU:6, one launch (start us, length us, event | category | flops | bytes accessed | tf_op | source)
XLA Modules:
  0.0 96.3 jit_solution(2198147570731670541)
XLA Ops:
  6.5 0.8 reshape.266.dest_ref
  7.3 0.8 reshape.267.aid_ref
  8.1 0.8 reshape.269.table_ref
  8.8 0.8 reshape.268.list_ref
  9.6 0.0 copy-start
  9.6 0.0 copy-start.1
  9.6 0.0 copy-start.3
  9.6 0.0 copy-start.4
  9.7 0.0 copy-start.6
  9.7 77.4 %fused.1 = (bf16[32,24,64]{2,1,0:T(8,128)(2,1)S(1)}, f32[8,128]{1,0:T(8,128)S(1)}) custom-call(bf16[256,1024]{1,0:T(8,128)(2,1)} %x_ref.1, bf16[1024,1024]{1,0:T(8,128)(2,1)} %v_ref.1, bf16[512,1024]{1,0:T(8,128)(2,1)} %bitcast.53, bf16[512,64]{1,0:T(8,128)(2,1)} %bitcast.54, s32[32,256]{1,0:T(8,128)S(1)} %reshape.266.dest_ref, ...), custom_call_target="tpu_custom_call" | custom-call | tf_op jit(solution)/shard_map/fused/pallas_call | solution.py:639
  87.1 0.6 reduce_max.9
  88.3 0.0 copy-done
  88.4 0.0 copy-done.1
  88.4 0.0 copy-done.3
  88.4 0.0 copy-done.4
  88.4 0.0 copy-done.6
  88.4 0.4 conditional.1
  88.4 0.1 copy.18
  88.8 0.0 copy-start.5
  88.8 0.6 copy-done.5
Async XLA Ops:
  9.6 78.7 %copy-start = (s32[1024]{0:T(1024)S(1)}, s32[1024]{0:T(1024)}, u32[]{:S(2)}) copy-start(s32[1024]{0:T(1024)} %param.17) | copy-start | bytes 12292
  9.6 78.7 %copy-start.1 = (bf16[32,16,1024]{2,1,0:T(8,128)(2,1)S(1)}, bf16[32,16,1024]{2,1,0:T(8,128)(2,1)}, u32[]{:S(2)}) copy-start(bf16[32,16,1024]{2,1,0:T(8,128)(2,1)} %param.12) | copy-start | bytes 3145732
  9.6 78.7 %copy-start.3 = (bf16[32,16,64]{2,1,0:T(8,128)(2,1)S(1)}, bf16[32,16,64]{2,1,0:T(8,128)(2,1)}, u32[]{:S(2)}) copy-start(bf16[32,16,64]{2,1,0:T(8,128)(2,1)} %param.13) | copy-start | bytes 196612
  9.6 78.7 %copy-start.4 = (s32[8192]{0:T(1024)S(1)}, s32[8192]{0:T(1024)}, u32[]{:S(2)}) copy-start(s32[8192]{0:T(1024)} %param.14) | copy-start | bytes 98308
  9.7 78.7 %copy-start.6 = (s32[32,32]{1,0:T(8,128)S(1)}, s32[32,32]{1,0:T(8,128)}, u32[]{:S(2)}) copy-start(s32[32,32]{1,0:T(8,128)} %param.16) | copy-start | bytes 12292
  88.8 0.6 copy-start.5

commit v2 on v1

--- a/solution.py
+++ b/solution.py
@@ -146,9 +146,9 @@
     mine_s,
     adp,
     back_pick,
-    fold,
     rs_send,
     rs_recv,
+    tile_sum,
     ag,
     xsend,
     xrecv,
@@ -167,7 +167,6 @@
     xrecv_sem,
     osend_sem,
     orecv_sem,
-    local_sem,
 ):
     me = lax.axis_index("rep")
     mt = lax.axis_index("tp")
@@ -176,42 +175,53 @@
     nz = groups // NX
     tok, depth = x_ref.shape
     part = depth // CHUNKS
-    homes = table_ref.shape[1]
-    cache = list_ref.shape[1] // groups
+    cache = list_ref.shape[1]
+    homes = table_ref.shape[0] * LANES // groups
     rank = a_ref.shape[0] // homes
+    rows_of = tok // LANES
     per = LANES // rank
     slots = NX * ROWS_X
     rowcap = out_ref.shape[1]
 
     barrier = pltpu.get_barrier_semaphore()
 
-    def greet_rep(k, c):
-        pl.semaphore_signal(
-            barrier, inc=1, device_id={"rep": lax.rem(me + k, groups)}, device_id_type=MESH
-        )
-        return c
-
-    def greet_tp(k, c):
-        pl.semaphore_signal(
-            barrier, inc=1, device_id={"tp": lax.rem(mt + k, peers)}, device_id_type=MESH
-        )
-        return c
-
-    lax.fori_loop(1, groups, greet_rep, 0)
-    lax.fori_loop(1, peers, greet_tp, 0)
+    def z_of(d):
+        return lax.rem(mz + d, nz)
+
+    def x_of(d):
+        return lax.rem(mx + d, NX)
+
+    def tp_of(d):
+        return lax.rem(mt + d, peers)
+
+    def greet(**where):
+        pl.semaphore_signal(barrier, inc=1, device_id=where, device_id_type=MESH)
+
+    z_steps = sorted(range(1, nz), key=lambda d: -min(d, nz - d))
+    for d in z_steps:
+        greet(rep=z_of(d) * NX + mx)
+    for d in range(1, peers):
+        greet(tp=tp_of(d))
+    for d in range(1, NX):
+        greet(rep=mz * NX + x_of(d))
 
     upper[...] = hot(iota((tok, tok), 0) < iota((tok, tok), 1))
 
-    listed = list_ref[...]
     count = groups * cache
+    lists = list_ref[...]
+    place_of = hot(iota((cache, count), 0) == iota((cache, count), 1) % cache)
+    owner = iota((groups, count), 1) // cache == iota((groups, count), 0)
+    high = jnp.where(owner, nn(hot_value(lists // LANES), place_of), 0.0)
+    low = jnp.where(owner, nn(hot_value(lists % LANES), place_of), 0.0)
+    high = jnp.sum(high, axis=0, keepdims=True).astype(I32)
+    low = jnp.sum(low, axis=0, keepdims=True).astype(I32)
     table = table_ref[...]
     both = jnp.concatenate([hot_value(table // homes), hot_value(table % homes)], axis=0)
-    major = iota((table.shape[0], count), 0) == listed // homes
-    minor = iota((homes, count), 0) == listed % homes
+    major = iota((table.shape[0], count), 0) == high
+    minor = iota((LANES, count), 0) == low
     found = nn(both, hot(minor))
     of_home = jnp.sum(jnp.where(major, found[: table.shape[0]], 0.0), axis=0, keepdims=True)
     of_local = jnp.sum(jnp.where(major, found[table.shape[0] :], 0.0), axis=0, keepdims=True)
-    owner = iota((groups, count), 1) // cache == iota((groups, count), 0)
     spread = jnp.concatenate(
         [jnp.where(owner, of_home, 0.0), jnp.where(owner, of_local, 0.0)], axis=0
     ).astype(BF16)
@@ -231,8 +241,11 @@
         earlier = nn(hot(member), upper[...])
         return jnp.sum(jnp.where(member, earlier, 0.0), axis=0, keepdims=True).astype(I32)
 
-    own_dest = dest_ref[pl.ds(me, 1), :]
-    own_home, _ = look_up(own_dest, aid_ref[pl.ds(me, 1), :])
+    def own(ref):
+        return jnp.concatenate([ref[pl.ds(rows_of * me + i, 1), :] for i in range(rows_of)], axis=1)
+
+    own_dest = own(dest_ref)
+    own_home, _ = look_up(own_dest, own(aid_ref))
     own_plane = own_home // NX
     own_rank1 = rank_in(iota((nz, tok), 0) == own_plane)
     own_slot1 = jnp.where(own_rank1 < ROWS_Z, own_plane * ROWS_Z + own_rank1, -1)
@@ -243,84 +256,45 @@
         send1[c] = rows.astype(BF16).reshape(nz, ROWS_Z, part)
 
     pack(0)
-    pl.semaphore_wait(barrier, groups + peers - 2)
-
-    def z_step(k):
-        return lax.rem(nz // 2 + (1 - 2 * lax.rem(k, 2)) * ((k + 1) // 2) + nz, nz)
-
-    def z_copy(c, to, frm):
-        return pltpu.make_async_remote_copy(
-            src_ref=send1.at[c, to],
-            dst_ref=recv1.at[c, frm],
-            send_sem=send1_sem.at[c, to],
-            recv_sem=recv1_sem.at[c, frm],
-            device_id={"rep": to * NX + mx},
+    pl.semaphore_wait(barrier, nz + NX + peers - 3)
+
+    def arrived(buffer, sem):
+        pltpu.make_async_copy(buffer, buffer, sem).wait()
+
+    def push(src, dst, ssem, rsem, **where):
+        pltpu.make_async_remote_copy(
+            src_ref=src,
+            dst_ref=dst,
+            send_sem=ssem,
+            recv_sem=rsem,
+            device_id=where,
             device_id_type=MESH,
-        )
-
-    def x_copy(c, to, frm):
-        return pltpu.make_async_remote_copy(
-            src_ref=send2.at[c, to],
-            dst_ref=recv2.at[c, frm],
-            send_sem=send2_sem.at[c, to],
-            recv_sem=recv2_sem.at[c, frm],
-            device_id={"rep": mz * NX + to},
-            device_id_type=MESH,
-        )
+        ).start()
 
     def z_start(c):
-        def body(k, w):
-            z_copy(c, lax.rem(mz + z_step(k), nz), mz).start()
-            return w
-
-        lax.fori_loop(0, nz - 1, body, 0)
+        for d in z_steps:
+            to = z_of(d)
+            push(
+                send1.at[c, to],
+                recv1.at[c, mz],
+                send1_sem.at[c],
+                recv1_sem.at[c],
+                rep=to * NX + mx,
+            )
+        pltpu.make_async_copy(send1.at[c, mz], recv1.at[c, mz], recv1_sem.at[c]).start()
 
     z_start(0)
     for c in range(1, CHUNKS):
         pack(c)
         z_start(c)
-    for c in range(CHUNKS):
-        recv1[c, mz] = send1[c, mz]
-
-    def target_of(k):
-        z = lax.rem(mz + z_step(k // NX), nz)
-        return z * NX + lax.rem(mx + 1 + lax.rem(k, NX), NX)
-
-    def source_of(k):
-        z = lax.rem(mz + nz - z_step(k // NX), nz)
-        return z * NX + lax.rem(mx + 2 * NX - 1 - lax.rem(k, NX), NX)
-
-    def rep_copy(src, dst, ssem, rsem, to, frm):
-        return pltpu.make_async_remote_copy(
-            src_ref=src.at[to],
-            dst_ref=dst.at[frm],
-            send_sem=ssem.at[to],
-            recv_sem=rsem.at[frm],
-            device_id={"rep": to},
-            device_id_type=MESH,
-        )
-
-    def start_rep(src, dst, ssem, rsem):
-        def body(k, w):
-            rep_copy(src, dst, ssem, rsem, target_of(k), me).start()
-            return w
-
-        lax.fori_loop(0, groups - 1, body, 0)
-
-    def finish_rep_send(src, dst, ssem, rsem):
-        def body(k, w):
-            rep_copy(src, dst, ssem, rsem, target_of(k), me).wait_send()
-            return w
-
-        lax.fori_loop(0, groups - 1, body, 0)
-
-    def finish_rep_recv(src, dst, ssem, rsem):
-        def body(k, w):
-            s = source_of(k)
-            rep_copy(src, dst, ssem, rsem, s, s).wait_recv()
-            return w
-
-        lax.fori_loop(0, groups - 1, body, 0)
+
+    def to_groups(src, dst, ssem, rsem):
+        for dz in z_steps + [0]:
+            for dx in range(NX):
+                if dz or dx:
+                    to = z_of(dz) * NX + x_of(dx)
+                    push(src.at[to], dst.at[me], ssem.at[0], rsem.at[0], rep=to)
+        pltpu.make_async_copy(src.at[me], dst.at[me], rsem.at[0]).start()
 
     width = bsend.shape[1]
     step = 256
@@ -329,28 +303,18 @@
         for i in range(step // width):
             bsend[n * (step // width) + i] = bt[i * width : (i + 1) * width]
 
-    def base_copy(to, frm):
-        return pltpu.make_async_remote_copy(
-            src_ref=bsend.at[to],
-            dst_ref=brecv.at[frm],
-            send_sem=bsend_sem.at[to],
-            recv_sem=brecv_sem.at[frm],
-            device_id={"tp": to},
-            device_id_type=MESH,
-        )
-
-    def base_start(k, w):
-        base_copy(lax.rem(mt + k, peers), mt).start()
-        return w
-
-    lax.fori_loop(1, peers, base_start, 0)
+    for d in range(1, peers):
+        to = tp_of(d)
+        push(bsend.at[to], brecv.at[mt], bsend_sem.at[0], brecv_sem.at[0], tp=to)
+    pltpu.make_async_copy(bsend.at[mt], brecv.at[mt], brecv_sem.at[0]).start()
 
     batch = 8
     counts = jnp.zeros((groups, LANES), F32)
     for q in range(groups // batch):
         ids = range(q * batch, (q + 1) * batch)
-        dest = jnp.concatenate([dest_ref[g : g + 1, :] for g in ids], axis=1)
-        aid = jnp.concatenate([aid_ref[g : g + 1, :] for g in ids], axis=1)
+        lines = range(q * batch * rows_of, (q + 1) * batch * rows_of)
+        dest = jnp.concatenate([dest_ref[r : r + 1, :] for r in lines], axis=1)
+        aid = jnp.concatenate([aid_ref[r : r + 1, :] for r in lines], axis=1)
         home, local = look_up(dest, aid)
         for j, g in enumerate(ids):
             home_s[g : g + 1, :] = home[:, j * tok : (j + 1) * tok]
@@ -369,7 +333,7 @@
         + jnp.max(jnp.where(by_plane > ROWS_Z, 1.0, 0.0), axis=0, keepdims=True)
         + jnp.max(jnp.where(by_column > ROWS_X, 1.0, 0.0), axis=0, keepdims=True)
     )
-    over_ref[...] = jnp.broadcast_to(over, over_ref.shape)
+    over_ref[0, 0] = jnp.max(over).astype(I32)
 
     homes_all = home_s[...]
     before = hot(
@@ -412,31 +376,25 @@
     acc[...] = jnp.zeros_like(acc)
 
     def shrink(c):
-        def wait_x(k, w):
-            frm = lax.rem(mx + k, NX)
-            x_copy(c, frm, frm).wait_recv()
-            return w
-
-        lax.fori_loop(1, NX, wait_x, 0)
+        arrived(recv2.at[c], recv2_sem.at[c])
         rows = recv2[c].reshape(slots, part)
         acc[...] += nt(rows, a_ref[:, c * part : (c + 1) * part])
 
     def stage(c):
-        def wait_z(k, w):
-            frm = lax.rem(mz + nz - z_step(k), nz)
-            z_copy(c, frm, frm).wait_recv()
-            return w
-
-        lax.fori_loop(0, nz - 1, wait_z, 0)
+        arrived(recv1.at[c], recv1_sem.at[c])
         rows = nn(pick2[...], recv1[c].reshape(nz * ROWS_Z, part))
         send2[c] = rows.astype(BF16).reshape(NX, ROWS_X, part)
 
-        def send_x(k, w):
-            x_copy(c, lax.rem(mx + k, NX), mx).start()
-            return w
-
-        lax.fori_loop(1, NX, send_x, 0)
-        recv2[c, mx] = send2[c, mx]
+        for d in range(1, NX):
+            to = x_of(d)
+            push(
+                send2.at[c, to],
+                recv2.at[c, mx],
+                send2_sem.at[c],
+                recv2_sem.at[c],
+                rep=mz * NX + to,
+            )
+        pltpu.make_async_copy(send2.at[c, mx], recv2.at[c, mx], recv2_sem.at[c]).start()
 
     def homed(g, w):
         column = lax.rem(g, NX)
@@ -454,7 +412,6 @@
         lax.fori_loop(c * quarter, (c + 1) * quarter, homed, 0)
         if c:
             shrink(c - 1)
-    column = jnp.broadcast_to(own_home.astype(F32), (LANES, tok))
     own_back = rank_in(iota((groups, tok), 0) == own_home)
     own_back = jnp.where(own_back < BACK, own_home * BACK + own_back, -1)
     column = jnp.broadcast_to(own_back.astype(F32), (LANES, tok)).T[:, 0:1].astype(I32)
@@ -477,64 +434,25 @@
             half * (t % 2) : half * (t % 2 + 1), (t // 2) * LANES : (t // 2 + 1) * LANES
         ]
 
-    def rs_copy(tile, frm):
-        return pltpu.make_async_remote_copy(
-            src_ref=rs_send.at[tile],
-            dst_ref=rs_recv.at[frm],
-            send_sem=rs_send_sem.at[tile],
-            recv_sem=rs_recv_sem.at[frm],
-            device_id={"tp": 2 * tile},
-            device_id_type=MESH,
-        )
-
-    def ag_copy(tile, to):
-        return pltpu.make_async_remote_copy(
-            src_ref=ag.at[tile],
-            dst_ref=ag.at[tile],
-            send_sem=ag_send_sem.at[to],
-            recv_sem=ag_recv_sem.at[tile],
-            device_id={"tp": to},
-            device_id_type=MESH,
-        )
-
-    def rs_start(k, w):
-        tile = lax.rem(my + tiles // 2 + k, tiles)
-
-        @pl.when(2 * tile != mt)
-        def _():
-            rs_copy(tile, mt).start()
-
-        return w
-
-    lax.fori_loop(0, tiles, rs_start, 0)
-
-    @pl.when(lax.rem(mt, 2) == 0)
+    first_core = lax.rem(mt, 2) == 0
+    for d in sorted(range(1, tiles), key=lambda d: -min(d, tiles - d)):
+        tile = lax.rem(my + d, tiles)
+        push(rs_send.at[tile], rs_recv.at[mt], rs_send_sem.at[0], rs_recv_sem.at[0], tp=2 * tile)
+
+    @pl.when(jnp.logical_not(first_core))
     def _():
-        rs_recv[mt] = rs_send[my]
-
-        def rs_wait(k, w):
-            rs_copy(my, lax.rem(mt + k, peers)).wait_recv()
-            return w
-
-        lax.fori_loop(1, peers, rs_wait, 0)
-        ag[my] = jnp.sum(rs_recv[...], axis=0)
-
-        def ag_start(k, w):
-            ag_copy(my, lax.rem(mt + k, peers)).start()
-            return w
-
-        lax.fori_loop(1, peers, ag_start, 0)
-
-    def ag_wait(k, w):
-        tile = lax.rem(my + k, tiles)
-
-        @pl.when(2 * tile != mt)
-        def _():
-            ag_copy(tile, mt).wait_recv()
-
-        return w
-
-    lax.fori_loop(0, tiles, ag_wait, 0)
+        push(rs_send.at[my], rs_recv.at[mt], rs_send_sem.at[0], rs_recv_sem.at[0], tp=2 * my)
+
+    @pl.when(first_core)
+    def _():
+        pltpu.make_async_copy(rs_send.at[my], rs_recv.at[mt], rs_recv_sem.at[0]).start()
+        arrived(rs_recv, rs_recv_sem.at[0])
+        tile_sum[...] = jnp.sum(rs_recv[...], axis=0)
+        for d in sorted(range(1, peers), key=lambda d: -min(d, peers - d)):
+            push(tile_sum, ag.at[my], ag_send_sem.at[0], ag_recv_sem.at[0], tp=tp_of(d))
+        pltpu.make_async_copy(tile_sum, ag.at[my], ag_recv_sem.at[0]).start()
+
+    arrived(ag, ag_recv_sem.at[0])
 
     e2 = jnp.concatenate([e_ref[...], e_ref[...]], axis=1)
     lane1 = iota((ROWS_X, LANES), 1)
@@ -557,72 +475,36 @@
         rows = nn(sel, pair)
         for z in range(nz):
             xsend[z * NX + y] = rows[z * BACK : (z + 1) * BACK].astype(BF16)
-    start_rep(xsend, xrecv, xsend_sem, xrecv_sem)
-    keep2 = pltpu.make_async_copy(xsend.at[me], xrecv.at[me], local_sem.at[0])
-    keep2.start()
-
-    def base_wait(k, w):
-        frm = lax.rem(mt + k, peers)
-        base_copy(frm, frm).wait_recv()
-        return w
-
-    lax.fori_loop(1, peers, base_wait, 0)
-    brecv[mt] = bsend[mt]
+    to_groups(xsend, xrecv, xsend_sem, xrecv_sem)
+
+    arrived(brecv, brecv_sem.at[0])
     base = jnp.sum(brecv[...], axis=0)
 
-    keep2.wait()
-    finish_rep_recv(xsend, xrecv, xsend_sem, xrecv_sem)
+    arrived(xrecv, xrecv_sem.at[0])
     extra = nn(unpack, xrecv[...].reshape(groups * BACK, LANES)).T
     total = (base + extra[:width] + extra[width:]).astype(BF16)
     final = nt(place_out, total)
     for s in range(groups):
         osend[s] = final[s * rowcap : (s + 1) * rowcap].astype(BF16)
-    start_rep(osend, out_ref, osend_sem, orecv_sem)
-    keep3 = pltpu.make_async_copy(osend.at[me], out_ref.at[me], local_sem.at[1])
-    keep3.start()
+    to_groups(osend, out_ref, osend_sem, orecv_sem)
 
     for c in range(CHUNKS):
-
-        def z_sent(k, w):
-            z_copy(c, lax.rem(mz + z_step(k), nz), mz).wait_send()
-            return w
-
-        def x_sent(k, w):
-            x_copy(c, lax.rem(mx + k, NX), mx).wait_send()
-            return w
-
-        lax.fori_loop(0, nz - 1, z_sent, 0)
-        lax.fori_loop(1, NX, x_sent, 0)
-
-    def base_sent(k, w):
-        base_copy(lax.rem(mt + k, peers), mt).wait_send()
-        return w
-
-    lax.fori_loop(1, peers, base_sent, 0)
-
-    def rs_sent(k, w):
-        tile = lax.rem(my + k, tiles)
-
-        @pl.when(2 * tile != mt)
-        def _():
-            rs_copy(tile, mt).wait_send()
-
-        return w
-
-    lax.fori_loop(0, tiles, rs_sent, 0)
-
-    @pl.when(lax.rem(mt, 2) == 0)
+        arrived(send1.at[c, pl.ds(0, nz - 1)], send1_sem.at[c])
+        arrived(send2.at[c, pl.ds(0, NX - 1)], send2_sem.at[c])
+    arrived(bsend.at[pl.ds(0, peers - 1)], bsend_sem.at[0])
+    arrived(rs_send.at[pl.ds(0, tiles - 1)], rs_send_sem.at[0])
+
+    @pl.when(jnp.logical_not(first_core))
     def _():
-        def ag_sent(k, w):
-            ag_copy(my, lax.rem(mt + k, peers)).wait_send()
-            return w
-
-        lax.fori_loop(1, peers, ag_sent, 0)
-
-    finish_rep_send(xsend, xrecv, xsend_sem, xrecv_sem)
-    keep3.wait()
-    finish_rep_send(osend, out_ref, osend_sem, orecv_sem)
-    finish_rep_recv(osend, out_ref, osend_sem, orecv_sem)
+        arrived(rs_send.at[0], rs_send_sem.at[0])
+
+    @pl.when(first_core)
+    def _():
+        arrived(rs_recv.at[pl.ds(0, peers - 1)], ag_send_sem.at[0])
+
+    arrived(xsend.at[pl.ds(0, groups - 1)], xsend_sem.at[0])
+    arrived(osend.at[pl.ds(0, groups - 1)], osend_sem.at[0])
+    arrived(out_ref, orecv_sem.at[0])
 
 
 def hot_value(a):
@@ -640,10 +522,10 @@
         functools.partial(fused_kernel, groups, peers),
         out_shape=[
             jax.ShapeDtypeStruct((groups, rowcap, width), BF16),
-            jax.ShapeDtypeStruct((8, LANES), F32),
+            jax.ShapeDtypeStruct((1, 1), I32),
         ],
         in_specs=[vmem] * 8,
-        out_specs=[vmem, vmem],
+        out_specs=[vmem, pl.BlockSpec(memory_space=pltpu.SMEM)],
         scratch_shapes=[
             pltpu.VMEM((CHUNKS, nz, ROWS_Z, part), BF16),
             pltpu.VMEM((CHUNKS, nz, ROWS_Z, part), BF16),
@@ -655,7 +537,7 @@
             pltpu.VMEM((nz * ROWS_Z, slots), F32),
             pltpu.VMEM((slots, nz * ROWS_Z), BF16),
             pltpu.VMEM((tok, tok), BF16),
-            pltpu.VMEM((2 * groups, lists.shape[1] // groups), BF16),
+            pltpu.VMEM((2 * groups, lists.shape[1]), BF16),
             pltpu.VMEM((groups, tok), I32),
             pltpu.VMEM((groups, tok), I32),
             pltpu.VMEM((groups, tok), I32),
@@ -663,28 +545,15 @@
             pltpu.VMEM((2, groups, tok), I32),
             pltpu.VMEM((slots, LANES), F32),
             pltpu.VMEM((NX, nz, BACK, LANES), F32),
-            pltpu.VMEM((slots, LANES), F32),
             pltpu.VMEM((peers // 2, 8, LANES), F32),
             pltpu.VMEM((peers, 8, LANES), F32),
+            pltpu.VMEM((8, LANES), F32),
             pltpu.VMEM((peers // 2, 8, LANES), F32),
             pltpu.VMEM((groups, BACK, LANES), BF16),
             pltpu.VMEM((groups, BACK, LANES), BF16),
             pltpu.VMEM((groups, rowcap, width), BF16),
-            dma((CHUNKS, nz)),
-            dma((CHUNKS, nz)),
-            dma((CHUNKS, NX)),
-            dma((CHUNKS, NX)),
-            dma((peers,)),
-            dma((peers,)),
-            dma((peers // 2,)),
-            dma((peers,)),
-            dma((peers,)),
-            dma((peers // 2,)),
-            dma((groups,)),
-            dma((groups,)),
-            dma((groups,)),
-            dma((groups,)),
-            dma((2,)),
+            *[dma((CHUNKS,))] * 4,
+            *[dma((1,))] * 10,
         ],
         compiler_params=pltpu.CompilerParams(
             collective_id=0, has_side_effects=True, vmem_limit_bytes=48 * 1024 * 1024
@@ -714,10 +583,10 @@
         value_weight,
         shrink_weight.reshape(home_count * rank, depth),
         expand_weight.reshape(home_count * rank, width),
-        destination.reshape(groups, tok),
-        adapter_ids.reshape(groups, tok),
-        cache_lists.reshape(1, -1),
-        home_table.reshape(-1, home_count),
+        destination.reshape(-1, LANES),
+        adapter_ids.reshape(-1, LANES),
+        cache_lists,
+        home_table.reshape(-1, LANES),
     )
     out = out.reshape(-1, width)
 
@@ -733,7 +602,7 @@
             home_table,
         )
 
-    return lax.cond(jnp.max(over) > 0.0, any_input, lambda out: out, out)
+    return lax.cond(over[0, 0] > 0, any_input, lambda out: out, out)
 
 
 def solution(mesh):

time: 97.8 us -> 91.5 us (0.936)
  local copies, waits for them, and re-layouts: 3.88 us -> 0.78 us
  Pallas kernels: 77.4 us -> 74.8 us
    reshape x4 -> x0, local copies, waits for them, and re-layouts: 3.09 us -> none  [the longest x1 0.8 us: on_device(): cache_lists.reshape(1, -1)]
    pallas_call x1, Pallas kernels: 77.4 us -> 74.8 us  [fused(): pl.pallas_call(functools.partial(fused_kernel, groups, peers), out_shape=...]
where the time goes in v2:
time: 91.5 us; the launch traced here: 89.9 us
  Pallas kernels  74.8 us (82%)
  between operations  14.1 us (15%)
    pallas_call x1, Pallas kernels, fused(): pl.pallas_call(functools.partial(fused_kernel, groups, peers), out_shape=...  74.8 us

profile of v2, /device:TPU:6, one launch (start us, length us, event | category | flops | bytes accessed | tf_op | source)
XLA Modules:
  0.0 89.9 jit_solution(13078351598368769430)
XLA Ops:
  6.5 0.0 copy-start
  6.5 0.0 copy-start.1
  6.5 0.0 copy-start.3
  6.5 0.0 copy-start.4
  6.5 0.0 copy-start.6
  6.5 74.8 %fused.1 = (bf16[32,24,64]{2,1,0:T(8,128)(2,1)S(1)}, s32[1,1]{1,0:T(1,128)}) custom-call(bf16[256,1024]{1,0:T(8,128)(2,1)} %x_ref.1, bf16[1024,1024]{1,0:T(8,128)(2,1)} %v_ref.1, bf16[512,1024]{1,0:T(8,128)(2,1)} %bitcast.58, bf16[512,64]{1,0:T(8,128)(2,1)} %bitcast.59, s32[64,128]{1,0:T(8,128)} %bitcast.60, s32[64,128]{1,0:T(8,128)} %bitcast.65, ...), custom_call_target="tpu_custom_call" | custom-call | tf_op jit(solution)/shard_map/fused/pallas_call | solution.py:521
  82.0 0.0 copy-done
  82.0 0.0 copy-done.1
  82.0 0.0 copy-done.3
  82.0 0.0 copy-done.4
  82.1 0.0 copy-done.6
  82.1 0.4 conditional.1
  82.1 0.1 copy.18
  82.4 0.0 copy-start.5
  82.5 0.6 copy-done.5
Async XLA Ops:
  6.5 75.5 %copy-start = (s32[1024]{0:T(1024)S(1)}, s32[1024]{0:T(1024)}, u32[]{:S(2)}) copy-start(s32[1024]{0:T(1024)} %param.17) | copy-start | bytes 12292
  6.5 75.5 %copy-start.1 = (bf16[32,16,1024]{2,1,0:T(8,128)(2,1)S(1)}, bf16[32,16,1024]{2,1,0:T(8,128)(2,1)}, u32[]{:S(2)}) copy-start(bf16[32,16,1024]{2,1,0:T(8,128)(2,1)} %param.12) | copy-start | bytes 3145732
  6.5 75.5 %copy-start.3 = (bf16[32,16,64]{2,1,0:T(8,128)(2,1)S(1)}, bf16[32,16,64]{2,1,0:T(8,128)(2,1)}, u32[]{:S(2)}) copy-start(bf16[32,16,64]{2,1,0:T(8,128)(2,1)} %param.13) | copy-start | bytes 196612
  6.5 75.5 %copy-start.4 = (s32[8192]{0:T(1024)S(1)}, s32[8192]{0:T(1024)}, u32[]{:S(2)}) copy-start(s32[8192]{0:T(1024)} %param.14) | copy-start | bytes 98308
  6.5 75.5 %copy-start.6 = (s32[32,32]{1,0:T(8,128)S(1)}, s32[32,32]{1,0:T(8,128)}, u32[]{:S(2)}) copy-start(s32[32,32]{1,0:T(8,128)} %list_ref.1) | copy-start | bytes 12292
  82.4 0.6 copy-start.5

commit v3 on v2

--- a/solution.py
+++ b/solution.py
@@ -94,8 +94,10 @@
 ROWS_Z = 64
 ROWS_X = 128
 BACK = 32
-CHUNKS = 4
+EIGHTHS = (3, 2, 2, 1)
+CHUNKS = len(EIGHTHS)
 LANES = 128
+TILE = 16
 F32, BF16, I32 = jnp.float32, jnp.bfloat16, jnp.int32
 
 
@@ -113,6 +115,11 @@
 
 def nt(a, b):
     return lax.dot_general(a, b, (((1,), (1,)), ((), ())), preferred_element_type=F32)
+
+
+def spans_of(depth):
+    ends = [depth * sum(EIGHTHS[:c]) // sum(EIGHTHS) for c in range(CHUNKS + 1)]
+    return list(zip(ends[:-1], ends[1:]))
 
 
 def fused_kernel(
@@ -153,6 +160,7 @@
     xsend,
     xrecv,
     osend,
+    orecv,
     send1_sem,
     recv1_sem,
     send2_sem,
@@ -174,7 +182,7 @@
     mz, mx = me // NX, me % NX
     nz = groups // NX
     tok, depth = x_ref.shape
-    part = depth // CHUNKS
+    spans = spans_of(depth)
     cache = list_ref.shape[1]
     homes = table_ref.shape[0] * LANES // groups
     rank = a_ref.shape[0] // homes
@@ -252,8 +260,9 @@
     pick1 = hot(iota((nz * ROWS_Z, tok), 0) == own_slot1)
 
     def pack(c):
-        rows = nn(pick1, x_ref[:, c * part : (c + 1) * part])
-        send1[c] = rows.astype(BF16).reshape(nz, ROWS_Z, part)
+        first, last = spans[c]
+        rows = nn(pick1, x_ref[:, first:last])
+        send1[c][...] = rows.astype(BF16).reshape(nz, ROWS_Z, last - first)
 
     pack(0)
     pl.semaphore_wait(barrier, nz + NX + peers - 3)
@@ -275,26 +284,18 @@
         for d in z_steps:
             to = z_of(d)
             push(
-                send1.at[c, to],
-                recv1.at[c, mz],
+                send1[c].at[to],
+                recv1[c].at[mz],
                 send1_sem.at[c],
                 recv1_sem.at[c],
                 rep=to * NX + mx,
             )
-        pltpu.make_async_copy(send1.at[c, mz], recv1.at[c, mz], recv1_sem.at[c]).start()
+        pltpu.make_async_copy(send1[c].at[mz], recv1[c].at[mz], recv1_sem.at[c]).start()
 
     z_start(0)
     for c in range(1, CHUNKS):
         pack(c)
         z_start(c)
-
-    def to_groups(src, dst, ssem, rsem):
-        for dz in z_steps + [0]:
-            for dx in range(NX):
-                if dz or dx:
-                    to = z_of(dz) * NX + x_of(dx)
-                    push(src.at[to], dst.at[me], ssem.at[0], rsem.at[0], rep=to)
-        pltpu.make_async_copy(src.at[me], dst.at[me], rsem.at[0]).start()
 
     width = bsend.shape[1]
     step = 256
@@ -376,25 +377,27 @@
     acc[...] = jnp.zeros_like(acc)
 
     def shrink(c):
-        arrived(recv2.at[c], recv2_sem.at[c])
-        rows = recv2[c].reshape(slots, part)
-        acc[...] += nt(rows, a_ref[:, c * part : (c + 1) * part])
+        arrived(recv2[c], recv2_sem.at[c])
+        first, last = spans[c]
+        rows = recv2[c][...].reshape(slots, last - first)
+        return nt(rows, a_ref[:, first:last])
 
     def stage(c):
-        arrived(recv1.at[c], recv1_sem.at[c])
-        rows = nn(pick2[...], recv1[c].reshape(nz * ROWS_Z, part))
-        send2[c] = rows.astype(BF16).reshape(NX, ROWS_X, part)
+        arrived(recv1[c], recv1_sem.at[c])
+        wide = spans[c][1] - spans[c][0]
+        rows = nn(pick2[...], recv1[c][...].reshape(nz * ROWS_Z, wide))
+        send2[c][...] = rows.astype(BF16).reshape(NX, ROWS_X, wide)
 
         for d in range(1, NX):
             to = x_of(d)
             push(
-                send2.at[c, to],
-                recv2.at[c, mx],
+                send2[c].at[to],
+                recv2[c].at[mx],
                 send2_sem.at[c],
                 recv2_sem.at[c],
                 rep=mz * NX + to,
             )
-        pltpu.make_async_copy(send2.at[c, mx], recv2.at[c, mx], recv2_sem.at[c]).start()
+        pltpu.make_async_copy(send2[c].at[mx], recv2[c].at[mx], recv2_sem.at[c]).start()
 
     def homed(g, w):
         column = lax.rem(g, NX)
@@ -406,25 +409,24 @@
         back_pick[column, g // NX] = nt(back, second)
         return w
 
-    quarter = groups // CHUNKS
+    shares = (0, 12 * groups // 32, 22 * groups // 32, groups, groups)
     for c in range(CHUNKS):
         stage(c)
-        lax.fori_loop(c * quarter, (c + 1) * quarter, homed, 0)
+        lax.fori_loop(shares[c], shares[c + 1], homed, 0)
         if c:
-            shrink(c - 1)
+            acc[...] += shrink(c - 1)
     own_back = rank_in(iota((groups, tok), 0) == own_home)
     own_back = jnp.where(own_back < BACK, own_home * BACK + own_back, -1)
     column = jnp.broadcast_to(own_back.astype(F32), (LANES, tok)).T[:, 0:1].astype(I32)
     unpack = hot(iota((tok, groups * BACK), 1) == column)
     own_out = own_dest * rowcap + rank_in(iota((groups, tok), 0) == own_dest)
-    place_out = hot(iota((groups * rowcap, tok), 0) == own_out)
-    shrink(CHUNKS - 1)
+    got = acc[...] + shrink(CHUNKS - 1)
 
     wanted = adp[...].astype(I32) - 1
     lane = iota((slots, LANES), 1) // rank
     folded = jnp.zeros((slots, LANES), F32)
     for n in range(homes // per):
-        folded += jnp.where(wanted == n * per + lane, acc[:, n * LANES : (n + 1) * LANES], 0.0)
+        folded += jnp.where(wanted == n * per + lane, got[:, n * LANES : (n + 1) * LANES], 0.0)
 
     low = jnp.sum(folded.T.reshape(per, rank, slots), axis=0)
     tiles = peers // 2
@@ -456,9 +458,10 @@
 
     e2 = jnp.concatenate([e_ref[...], e_ref[...]], axis=1)
     lane1 = iota((ROWS_X, LANES), 1)
-    for y in range(NX):
+    for dx in (2, 1, 3, 0):
+        y = x_of(dx)
         tile = jnp.concatenate([ag[2 * y], ag[2 * y + 1]] * per, axis=0).T
-        chosen = wanted[y * ROWS_X : (y + 1) * ROWS_X]
+        chosen = adp[pl.ds(pl.multiple_of(y * ROWS_X, ROWS_X), ROWS_X), :].astype(I32) - 1
         spread = jnp.concatenate(
             [
                 jnp.where(chosen == n * per + lane1 // rank, tile, 0.0)
@@ -475,7 +478,11 @@
         rows = nn(sel, pair)
         for z in range(nz):
             xsend[z * NX + y] = rows[z * BACK : (z + 1) * BACK].astype(BF16)
-    to_groups(xsend, xrecv, xsend_sem, xrecv_sem)
+        for dz in z_steps + [0]:
+            if dz or dx:
+                to = z_of(dz) * NX + y
+                push(xsend.at[to], xrecv.at[me], xsend_sem.at[0], xrecv_sem.at[0], rep=to)
+    pltpu.make_async_copy(xsend.at[me], xrecv.at[me], xrecv_sem.at[0]).start()
 
     arrived(brecv, brecv_sem.at[0])
     base = jnp.sum(brecv[...], axis=0)
@@ -483,14 +490,27 @@
     arrived(xrecv, xrecv_sem.at[0])
     extra = nn(unpack, xrecv[...].reshape(groups * BACK, LANES)).T
     total = (base + extra[:width] + extra[width:]).astype(BF16)
-    final = nt(place_out, total)
-    for s in range(groups):
-        osend[s] = final[s * rowcap : (s + 1) * rowcap].astype(BF16)
-    to_groups(osend, out_ref, osend_sem, orecv_sem)
+    blank = jnp.zeros_like(total)
+    sides = jnp.concatenate(
+        [jnp.concatenate([total, blank], axis=1), jnp.concatenate([blank, total], axis=1)], axis=0
+    )
+    line = iota((NX * TILE, tok), 0)
+    for dz in z_steps + [0]:
+        z = z_of(dz)
+        slot = z * NX * rowcap + line // TILE * rowcap + line % TILE
+        high = (slot + TILE == own_out) & (line % TILE < rowcap - TILE)
+        rows = nt(jnp.concatenate([hot(slot == own_out), hot(high)], axis=1), sides)
+        for i in range(NX):
+            osend[z * NX + i] = rows[i * TILE : (i + 1) * TILE].astype(BF16)
+        for dx in range(NX):
+            if dz or dx:
+                to = z * NX + x_of(dx)
+                push(osend.at[to], orecv.at[me], osend_sem.at[0], orecv_sem.at[0], rep=to)
+    pltpu.make_async_copy(osend.at[me], orecv.at[me], orecv_sem.at[0]).start()
 
     for c in range(CHUNKS):
-        arrived(send1.at[c, pl.ds(0, nz - 1)], send1_sem.at[c])
-        arrived(send2.at[c, pl.ds(0, NX - 1)], send2_sem.at[c])
+        arrived(send1[c].at[pl.ds(0, nz - 1)], send1_sem.at[c])
+        arrived(send2[c].at[pl.ds(0, NX - 1)], send2_sem.at[c])
     arrived(bsend.at[pl.ds(0, peers - 1)], bsend_sem.at[0])
     arrived(rs_send.at[pl.ds(0, tiles - 1)], rs_send_sem.at[0])
 
@@ -504,7 +524,10 @@
 
     arrived(xsend.at[pl.ds(0, groups - 1)], xsend_sem.at[0])
     arrived(osend.at[pl.ds(0, groups - 1)], osend_sem.at[0])
-    arrived(out_ref, orecv_sem.at[0])
+    arrived(orecv, orecv_sem.at[0])
+    done = orecv[...].astype(F32)
+    out_ref[:, :TILE, :] = done[:, :, :width].astype(BF16)
+    out_ref[:, TILE:, :] = done[:, : rowcap - TILE, width:].astype(BF16)
 
 
 def hot_value(a):
@@ -515,7 +538,8 @@
     tok, depth = requests.shape
     width = expand.shape[1]
     rowcap = 3 * tok // groups
-    nz, part, slots = groups // NX, depth // CHUNKS, NX * ROWS_X
+    nz, slots = groups // NX, NX * ROWS_X
+    wide = [last - first for first, last in spans_of(depth)]
     vmem = pl.BlockSpec(memory_space=pltpu.VMEM)
     dma = pltpu.SemaphoreType.DMA
     return pl.pallas_call(
@@ -527,10 +551,10 @@
         in_specs=[vmem] * 8,
         out_specs=[vmem, pl.BlockSpec(memory_space=pltpu.SMEM)],
         scratch_shapes=[
-            pltpu.VMEM((CHUNKS, nz, ROWS_Z, part), BF16),
-            pltpu.VMEM((CHUNKS, nz, ROWS_Z, part), BF16),
-            pltpu.VMEM((CHUNKS, NX, ROWS_X, part), BF16),
-            pltpu.VMEM((CHUNKS, NX, ROWS_X, part), BF16),
+            [pltpu.VMEM((nz, ROWS_Z, n), BF16) for n in wide],
+            [pltpu.VMEM((nz, ROWS_Z, n), BF16) for n in wide],
+            [pltpu.VMEM((NX, ROWS_X, n), BF16) for n in wide],
+            [pltpu.VMEM((NX, ROWS_X, n), BF16) for n in wide],
             pltpu.VMEM((peers, width, tok), F32),
             pltpu.VMEM((peers, width, tok), F32),
             pltpu.VMEM((slots, shrink.shape[0]), F32),
@@ -551,7 +575,8 @@
             pltpu.VMEM((peers // 2, 8, LANES), F32),
             pltpu.VMEM((groups, BACK, LANES), BF16),
             pltpu.VMEM((groups, BACK, LANES), BF16),
-            pltpu.VMEM((groups, rowcap, width), BF16),
+            pltpu.VMEM((groups, TILE, LANES), BF16),
+            pltpu.VMEM((groups, TILE, LANES), BF16),
             *[dma((CHUNKS,))] * 4,
             *[dma((1,))] * 10,
         ],

time: 91.5 us -> 88.1 us (0.963); the launches traced: 89.9 us -> 87.7 us
  Pallas kernels: 74.8 us -> 72.6 us
    pallas_call x1, Pallas kernels: 74.8 us -> 72.6 us  [fused(): pl.pallas_call(functools.partial(fused_kernel, groups, peers), out_shape=...]
where the time goes in v3:
time: 88.1 us; the launch traced here: 87.7 us
  Pallas kernels  72.6 us (82%)
  between operations  14.1 us (16%)
    pallas_call x1, Pallas kernels, fused(): pl.pallas_call(functools.partial(fused_kernel, groups, peers), out_shape=...  72.6 us

profile of v3, /device:TPU:6, one launch (start us, length us, event | category | flops | bytes accessed | tf_op | source)
XLA Modules:
  0.0 87.7 jit_solution(17390683990704591674)
XLA Ops:
  6.5 0.0 copy-start
  6.5 0.0 copy-start.1
  6.5 0.0 copy-start.3
  6.5 0.0 copy-start.4
  6.5 0.0 copy-start.6
  6.5 72.6 %fused.1 = (bf16[32,24,64]{2,1,0:T(8,128)(2,1)S(1)}, s32[1,1]{1,0:T(1,128)}) custom-call(bf16[256,1024]{1,0:T(8,128)(2,1)} %x_ref.1, bf16[1024,1024]{1,0:T(8,128)(2,1)} %v_ref.1, bf16[512,1024]{1,0:T(8,128)(2,1)} %bitcast.58, bf16[512,64]{1,0:T(8,128)(2,1)} %bitcast.59, s32[64,128]{1,0:T(8,128)} %bitcast.60, s32[64,128]{1,0:T(8,128)} %bitcast.65, ...), custom_call_target="tpu_custom_call" | custom-call | tf_op jit(solution)/shard_map/fused/pallas_call | solution.py:545
  79.8 0.0 copy-done
  79.9 0.0 copy-done.1
  79.9 0.0 copy-done.3
  79.9 0.0 copy-done.4
  79.9 0.0 copy-done.6
  79.9 0.4 conditional.1
  79.9 0.1 copy.18
  80.3 0.0 copy-start.5
  80.3 0.6 copy-done.5
Async XLA Ops:
  6.5 73.3 %copy-start = (s32[1024]{0:T(1024)S(1)}, s32[1024]{0:T(1024)}, u32[]{:S(2)}) copy-start(s32[1024]{0:T(1024)} %param.17) | copy-start | bytes 12292
  6.5 73.3 %copy-start.1 = (bf16[32,16,1024]{2,1,0:T(8,128)(2,1)S(1)}, bf16[32,16,1024]{2,1,0:T(8,128)(2,1)}, u32[]{:S(2)}) copy-start(bf16[32,16,1024]{2,1,0:T(8,128)(2,1)} %param.12) | copy-start | bytes 3145732
  6.5 73.3 %copy-start.3 = (bf16[32,16,64]{2,1,0:T(8,128)(2,1)S(1)}, bf16[32,16,64]{2,1,0:T(8,128)(2,1)}, u32[]{:S(2)}) copy-start(bf16[32,16,64]{2,1,0:T(8,128)(2,1)} %param.13) | copy-start | bytes 196612
  6.5 73.3 %copy-start.4 = (s32[8192]{0:T(1024)S(1)}, s32[8192]{0:T(1024)}, u32[]{:S(2)}) copy-start(s32[8192]{0:T(1024)} %param.14) | copy-start | bytes 98308
  6.5 73.3 %copy-start.6 = (s32[32,32]{1,0:T(8,128)S(1)}, s32[32,32]{1,0:T(8,128)}, u32[]{:S(2)}) copy-start(s32[32,32]{1,0:T(8,128)} %list_ref.1) | copy-start | bytes 12292
  80.3 0.6 copy-start.5

commit v4 on v3

--- a/solution.py
+++ b/solution.py
@@ -79,13 +79,19 @@
     shrunk_part = jnp.sum(
         shrunk_all.reshape(buffer_rows, cache_len, rank_width) * selector[:, :, None], axis=1
     )
-    shrunk = lax.psum(shrunk_part, "tp")
+    peers = lax.axis_size("tp")
+    pieces = lax.all_to_all(shrunk_part, "tp", split_axis=0, concat_axis=0, tiled=True)
+    piece = jnp.sum(pieces.reshape(peers, -1, rank_width), axis=0)
+    shrunk = lax.all_to_all(
+        jnp.tile(piece, (peers, 1)), "tp", split_axis=0, concat_axis=0, tiled=True
+    )
     spread_rows = (selector[:, :, None] * shrunk[:, None, :]).reshape(
         buffer_rows, cache_len * rank_width
     )
     expanded = jnp.dot(spread_rows, cached_up, precision=lax.Precision.HIGHEST)
     partial_all = jnp.dot(arrived, value_weight, preferred_element_type=jnp.float32)
-    projected = lax.psum_scatter(partial_all, "tp", scatter_dimension=1, tiled=True)
+    columns = lax.all_to_all(partial_all, "tp", split_axis=1, concat_axis=0, tiled=True)
+    projected = jnp.sum(columns.reshape(peers, buffer_rows, width_out), axis=0)
     return (projected + expanded).astype(jnp.bfloat16)
 
 
@@ -98,6 +104,7 @@
 CHUNKS = len(EIGHTHS)
 LANES = 128
 TILE = 16
+NEAR = 4
 F32, BF16, I32 = jnp.float32, jnp.bfloat16, jnp.int32
 
 
@@ -153,10 +160,11 @@
     mine_s,
     adp,
     back_pick,
-    rs_send,
-    rs_recv,
-    tile_sum,
-    ag,
+    far_src,
+    far,
+    near_src,
+    near,
+    low_sum,
     xsend,
     xrecv,
     osend,
@@ -167,10 +175,10 @@
     recv2_sem,
     bsend_sem,
     brecv_sem,
-    rs_send_sem,
-    rs_recv_sem,
-    ag_send_sem,
-    ag_recv_sem,
+    far_send_sem,
+    far_recv_sem,
+    near_send_sem,
+    near_recv_sem,
     xsend_sem,
     xrecv_sem,
     osend_sem,
@@ -178,7 +186,6 @@
 ):
     me = lax.axis_index("rep")
     mt = lax.axis_index("tp")
-    my = mt // 2
     mz, mx = me // NX, me % NX
     nz = groups // NX
     tok, depth = x_ref.shape
@@ -429,38 +436,28 @@
         folded += jnp.where(wanted == n * per + lane, got[:, n * LANES : (n + 1) * LANES], 0.0)
 
     low = jnp.sum(folded.T.reshape(per, rank, slots), axis=0)
-    tiles = peers // 2
-    half = rank // 2
-    for t in range(tiles):
-        rs_send[t] = low[
-            half * (t % 2) : half * (t % 2 + 1), (t // 2) * LANES : (t // 2 + 1) * LANES
-        ]
-
-    first_core = lax.rem(mt, 2) == 0
-    for d in sorted(range(1, tiles), key=lambda d: -min(d, tiles - d)):
-        tile = lax.rem(my + d, tiles)
-        push(rs_send.at[tile], rs_recv.at[mt], rs_send_sem.at[0], rs_recv_sem.at[0], tp=2 * tile)
-
-    @pl.when(jnp.logical_not(first_core))
-    def _():
-        push(rs_send.at[my], rs_recv.at[mt], rs_send_sem.at[0], rs_recv_sem.at[0], tp=2 * my)
-
-    @pl.when(first_core)
-    def _():
-        pltpu.make_async_copy(rs_send.at[my], rs_recv.at[mt], rs_recv_sem.at[0]).start()
-        arrived(rs_recv, rs_recv_sem.at[0])
-        tile_sum[...] = jnp.sum(rs_recv[...], axis=0)
-        for d in sorted(range(1, peers), key=lambda d: -min(d, peers - d)):
-            push(tile_sum, ag.at[my], ag_send_sem.at[0], ag_recv_sem.at[0], tp=tp_of(d))
-        pltpu.make_async_copy(tile_sum, ag.at[my], ag_recv_sem.at[0]).start()
-
-    arrived(ag, ag_recv_sem.at[0])
+    for i in range(NX):
+        far_src[i] = low[:, i * LANES : (i + 1) * LANES]
+    team = NEAR
+    for k in sorted(range(1, peers // team), key=lambda k: -min(k, peers // team - k)):
+        to = tp_of(team * k)
+        push(far_src, far.at[mt // team], far_send_sem.at[0], far_recv_sem.at[0], tp=to)
+    pltpu.make_async_copy(far_src, far.at[mt // team], far_recv_sem.at[0]).start()
+    arrived(far, far_recv_sem.at[0])
+    near_src[...] = jnp.sum(far[...], axis=0)
+    first = mt // team * team
+    for k in range(1, team):
+        to = first + lax.rem(mt + k, team)
+        push(near_src, near.at[mt - first], near_send_sem.at[0], near_recv_sem.at[0], tp=to)
+    pltpu.make_async_copy(near_src, near.at[mt - first], near_recv_sem.at[0]).start()
+    arrived(near, near_recv_sem.at[0])
+    low_sum[...] = jnp.sum(near[...], axis=0)
 
     e2 = jnp.concatenate([e_ref[...], e_ref[...]], axis=1)
     lane1 = iota((ROWS_X, LANES), 1)
     for dx in (2, 1, 3, 0):
         y = x_of(dx)
-        tile = jnp.concatenate([ag[2 * y], ag[2 * y + 1]] * per, axis=0).T
+        tile = jnp.concatenate([low_sum[y]] * per, axis=0).T
         chosen = adp[pl.ds(pl.multiple_of(y * ROWS_X, ROWS_X), ROWS_X), :].astype(I32) - 1
         spread = jnp.concatenate(
             [
@@ -512,16 +509,8 @@
         arrived(send1[c].at[pl.ds(0, nz - 1)], send1_sem.at[c])
         arrived(send2[c].at[pl.ds(0, NX - 1)], send2_sem.at[c])
     arrived(bsend.at[pl.ds(0, peers - 1)], bsend_sem.at[0])
-    arrived(rs_send.at[pl.ds(0, tiles - 1)], rs_send_sem.at[0])
-
-    @pl.when(jnp.logical_not(first_core))
-    def _():
-        arrived(rs_send.at[0], rs_send_sem.at[0])
-
-    @pl.when(first_core)
-    def _():
-        arrived(rs_recv.at[pl.ds(0, peers - 1)], ag_send_sem.at[0])
-
+    arrived(far.at[pl.ds(0, peers // team - 1)], far_send_sem.at[0])
+    arrived(near.at[pl.ds(0, team - 1)], near_send_sem.at[0])
     arrived(xsend.at[pl.ds(0, groups - 1)], xsend_sem.at[0])
     arrived(osend.at[pl.ds(0, groups - 1)], osend_sem.at[0])
     arrived(orecv, orecv_sem.at[0])
@@ -539,6 +528,7 @@
     width = expand.shape[1]
     rowcap = 3 * tok // groups
     nz, slots = groups // NX, NX * ROWS_X
+    rank = shrink.shape[0] * groups // (table.size)
     wide = [last - first for first, last in spans_of(depth)]
     vmem = pl.BlockSpec(memory_space=pltpu.VMEM)
     dma = pltpu.SemaphoreType.DMA
@@ -569,10 +559,11 @@
             pltpu.VMEM((2, groups, tok), I32),
             pltpu.VMEM((slots, LANES), F32),
             pltpu.VMEM((NX, nz, BACK, LANES), F32),
-            pltpu.VMEM((peers // 2, 8, LANES), F32),
-            pltpu.VMEM((peers, 8, LANES), F32),
-            pltpu.VMEM((8, LANES), F32),
-            pltpu.VMEM((peers // 2, 8, LANES), F32),
+            pltpu.VMEM((NX, rank, LANES), F32),
+            pltpu.VMEM((peers // NEAR, NX, rank, LANES), F32),
+            pltpu.VMEM((NX, rank, LANES), F32),
+            pltpu.VMEM((NEAR, NX, rank, LANES), F32),
+            pltpu.VMEM((NX, rank, LANES), F32),
             pltpu.VMEM((groups, BACK, LANES), BF16),
             pltpu.VMEM((groups, BACK, LANES), BF16),
             pltpu.VMEM((groups, TILE, LANES), BF16),

time: 88.1 us -> 74 us (0.84)
  between operations: 14.1 us -> 0.79 us
  Pallas kernels: 72.6 us -> 71.3 us
    pallas_call x1, Pallas kernels: 72.6 us -> 71.3 us  [fused(): pl.pallas_call(functools.partial(fused_kernel, groups, peers), out_shape=...]
where the time goes in v4:
time: 74 us; the launch traced here: 73.1 us
  Pallas kernels  71.3 us (96%)
  local copies, waits for them, and re-layouts  0.79 us (1%)
  between operations  0.79 us (1%)
    pallas_call x1, Pallas kernels, fused(): pl.pallas_call(functools.partial(fused_kernel, groups, peers), out_shape=...  71.3 us

profile of v4, /device:TPU:6, one launch (start us, length us, event | category | flops | bytes accessed | tf_op | source)
XLA Modules:
  0.0 73.1 jit_solution(15609572507861039798)
XLA Ops:
  0.0 0.0 copy-start
  0.0 0.0 copy-start.1
  0.0 0.0 copy-start.2
  0.0 0.0 copy-start.3
  0.0 0.0 copy-start.4
  0.0 0.0 copy-start.14
  0.0 71.3 %fused.1 = (bf16[32,24,64]{2,1,0:T(8,128)(2,1)S(1)}, s32[1,1]{1,0:T(1,128)}) custom-call(bf16[256,1024]{1,0:T(8,128)(2,1)} %x_ref.1, bf16[1024,1024]{1,0:T(8,128)(2,1)} %v_ref.1, bf16[512,1024]{1,0:T(8,128)(2,1)} %bitcast.77, bf16[512,64]{1,0:T(8,128)(2,1)} %bitcast.80, s32[64,128]{1,0:T(8,128)} %bitcast.81, s32[64,128]{1,0:T(8,128)} %bitcast.88, ...), custom_call_target="tpu_custom_call" | custom-call | tf_op jit(solution)/shard_map/fused/pallas_call | solution.py:535
  72.0 0.0 copy-done
  72.0 0.0 copy-done.1
  72.0 0.0 copy-done.2
  72.0 0.0 copy-done.3
  72.0 0.0 copy-done.4
  72.0 0.0 copy-done.14
  72.0 0.4 conditional.1
  72.1 0.1 copy.46
  72.4 0.0 copy-start.13
  72.4 0.6 copy-done.13
Async XLA Ops:
  0.0 72.0 %copy-start = (s32[1024]{0:T(1024)S(1)}, s32[1024]{0:T(1024)}, u32[]{:S(2)}) copy-start(s32[1024]{0:T(1024)} %param.17) | copy-start | bytes 12292
  0.0 72.0 %copy-start.1 = (bf16[32,16,1024]{2,1,0:T(8,128)(2,1)S(1)}, bf16[32,16,1024]{2,1,0:T(8,128)(2,1)}, u32[]{:S(2)}) copy-start(bf16[32,16,1024]{2,1,0:T(8,128)(2,1)} %param.12) | copy-start | bytes 3145732
  0.0 72.0 %copy-start.2 = (bf16[1024,1024]{1,0:T(8,128)(2,1)S(1)}, bf16[1024,1024]{1,0:T(8,128)(2,1)}, u32[]{:S(2)}) copy-start(bf16[1024,1024]{1,0:T(8,128)(2,1)} %v_ref.1) | copy-start | bytes 6291460
  0.0 72.0 %copy-start.3 = (bf16[32,16,64]{2,1,0:T(8,128)(2,1)S(1)}, bf16[32,16,64]{2,1,0:T(8,128)(2,1)}, u32[]{:S(2)}) copy-start(bf16[32,16,64]{2,1,0:T(8,128)(2,1)} %param.13) | copy-start | bytes 196612
  0.0 72.0 %copy-start.4 = (s32[8192]{0:T(1024)S(1)}, s32[8192]{0:T(1024)}, u32[]{:S(2)}) copy-start(s32[8192]{0:T(1024)} %param.14) | copy-start | bytes 98308
  0.0 72.0 %copy-start.14 = (s32[32,32]{1,0:T(8,128)S(1)}, s32[32,32]{1,0:T(8,128)}, u32[]{:S(2)}) copy-start(s32[32,32]{1,0:T(8,128)} %list_ref.1) | copy-start | bytes 12292
  72.4 0.6 copy-start.13

commit v5 on v4

--- a/solution.py
+++ b/solution.py
@@ -132,16 +132,20 @@
 def fused_kernel(
     groups,
     peers,
-    x_ref,
-    v_ref,
-    a_ref,
-    e_ref,
+    x_hbm,
+    v_hbm,
+    a_hbm,
+    e_hbm,
     dest_ref,
     aid_ref,
     list_ref,
     table_ref,
     out_ref,
     over_ref,
+    x_ref,
+    v_ref,
+    a_ref,
+    e_ref,
     send1,
     recv1,
     send2,
@@ -183,6 +187,7 @@
     xrecv_sem,
     osend_sem,
     orecv_sem,
+    load_sem,
 ):
     me = lax.axis_index("rep")
     mt = lax.axis_index("tp")
@@ -197,6 +202,15 @@
     per = LANES // rank
     slots = NX * ROWS_X
     rowcap = out_ref.shape[1]
+
+    loads = [
+        pltpu.make_async_copy(src, dst, load_sem.at[i])
+        for i, (src, dst) in enumerate(
+            [(x_hbm, x_ref), (v_hbm, v_ref), (a_hbm, a_ref), (e_hbm, e_ref)]
+        )
+    ]
+    for load in loads:
+        load.start()
 
     barrier = pltpu.get_barrier_semaphore()
 
@@ -271,6 +285,7 @@
         rows = nn(pick1, x_ref[:, first:last])
         send1[c][...] = rows.astype(BF16).reshape(nz, ROWS_Z, last - first)
 
+    loads[0].wait()
     pack(0)
     pl.semaphore_wait(barrier, nz + NX + peers - 3)
 
@@ -305,6 +320,7 @@
         z_start(c)
 
     width = bsend.shape[1]
+    loads[1].wait()
     step = 256
     for n in range(v_ref.shape[1] // step):
         bt = nn(x_ref[...], v_ref[:, n * step : (n + 1) * step]).T
@@ -380,6 +396,8 @@
     lax.fori_loop(0, nz, route, 0)
     pick2[...] = pick2t[...].T.astype(BF16)
 
+    loads[2].wait()
+    loads[3].wait()
     adp[...] = jnp.zeros_like(adp)
     acc[...] = jnp.zeros_like(acc)
 
@@ -538,9 +556,13 @@
             jax.ShapeDtypeStruct((groups, rowcap, width), BF16),
             jax.ShapeDtypeStruct((1, 1), I32),
         ],
-        in_specs=[vmem] * 8,
+        in_specs=[pl.BlockSpec(memory_space=pl.ANY)] * 4 + [vmem] * 4,
         out_specs=[vmem, pl.BlockSpec(memory_space=pltpu.SMEM)],
         scratch_shapes=[
+            pltpu.VMEM(requests.shape, BF16),
+            pltpu.VMEM(value_weight.shape, BF16),
+            pltpu.VMEM(shrink.shape, BF16),
+            pltpu.VMEM(expand.shape, BF16),
             [pltpu.VMEM((nz, ROWS_Z, n), BF16) for n in wide],
             [pltpu.VMEM((nz, ROWS_Z, n), BF16) for n in wide],
             [pltpu.VMEM((NX, ROWS_X, n), BF16) for n in wide],
@@ -570,9 +592,10 @@
             pltpu.VMEM((groups, TILE, LANES), BF16),
             *[dma((CHUNKS,))] * 4,
             *[dma((1,))] * 10,
+            dma((4,)),
         ],
         compiler_params=pltpu.CompilerParams(
-            collective_id=0, has_side_effects=True, vmem_limit_bytes=48 * 1024 * 1024
+            collective_id=0, has_side_effects=True, vmem_limit_bytes=63 * 1024 * 1024
         ),
         name="fused",
     )(requests, value_weight, shrink, expand, dest, aid, lists, table)

time: 74 us -> 72.4 us (0.978)
  Pallas kernels: 71.3 us -> 69.8 us
    pallas_call x1, Pallas kernels: 71.3 us -> 69.8 us  [fused(): pl.pallas_call(functools.partial(fused_kernel, groups, peers), out_shape=...]
where the time goes in v5:
time: 72.4 us; the launch traced here: 71.6 us
  Pallas kernels  69.8 us (96%)
  local copies, waits for them, and re-layouts  0.78 us (1%)
  between operations  0.76 us (1%)
    pallas_call x1, Pallas kernels, fused(): pl.pallas_call(functools.partial(fused_kernel, groups, peers), out_shape=...  69.8 us

profile of v5, /device:TPU:6, one launch (start us, length us, event | category | flops | bytes accessed | tf_op | source)
XLA Modules:
  0.0 71.6 jit_solution(12883786141466415702)
XLA Ops:
  0.0 0.0 copy-start
  0.0 0.0 copy-start.3
  0.0 0.0 copy-start.4
  0.0 0.0 copy-start.11
  0.0 69.8 %fused.1 = (bf16[32,24,64]{2,1,0:T(8,128)(2,1)S(1)}, s32[1,1]{1,0:T(1,128)}) custom-call(bf16[256,1024]{1,0:T(8,128)(2,1)} %x_hbm.1, bf16[1024,1024]{1,0:T(8,128)(2,1)} %v_hbm.1, bf16[512,1024]{1,0:T(8,128)(2,1)} %bitcast.77, bf16[512,64]{1,0:T(8,128)(2,1)} %bitcast.79, s32[64,128]{1,0:T(8,128)} %bitcast.80, s32[64,128]{1,0:T(8,128)} %bitcast.87, ...), custom_call_target="tpu_custom_call" | custom-call | tf_op jit(solution)/shard_map/fused/pallas_call | solution.py:553
  70.6 0.0 copy-done
  70.6 0.0 copy-done.3
  70.6 0.0 copy-done.4
  70.6 0.0 copy-done.11
  70.6 0.4 conditional.1
  70.6 0.1 copy.46
  71.0 0.0 copy-start.10
  71.0 0.6 copy-done.10
Async XLA Ops:
  0.0 70.6 %copy-start = (s32[1024]{0:T(1024)S(1)}, s32[1024]{0:T(1024)}, u32[]{:S(2)}) copy-start(s32[1024]{0:T(1024)} %param.17) | copy-start | bytes 12292
  0.0 70.6 %copy-start.3 = (bf16[32,16,64]{2,1,0:T(8,128)(2,1)S(1)}, bf16[32,16,64]{2,1,0:T(8,128)(2,1)}, u32[]{:S(2)}) copy-start(bf16[32,16,64]{2,1,0:T(8,128)(2,1)} %param.13) | copy-start | bytes 196612
  0.0 70.6 %copy-start.4 = (s32[8192]{0:T(1024)S(1)}, s32[8192]{0:T(1024)}, u32[]{:S(2)}) copy-start(s32[8192]{0:T(1024)} %param.14) | copy-start | bytes 98308
  0.0 70.6 %copy-start.11 = (s32[32,32]{1,0:T(8,128)S(1)}, s32[32,32]{1,0:T(8,128)}, u32[]{:S(2)}) copy-start(s32[32,32]{1,0:T(8,128)} %list_ref.1) | copy-start | bytes 12292
  71.0 0.6 copy-start.10

commit v6 on v5

--- a/solution.py
+++ b/solution.py
@@ -163,6 +163,7 @@
     slot2_s,
     mine_s,
     adp,
+    early,
     back_pick,
     far_src,
     far,
@@ -445,13 +446,17 @@
     column = jnp.broadcast_to(own_back.astype(F32), (LANES, tok)).T[:, 0:1].astype(I32)
     unpack = hot(iota((tok, groups * BACK), 1) == column)
     own_out = own_dest * rowcap + rank_in(iota((groups, tok), 0) == own_dest)
-    got = acc[...] + shrink(CHUNKS - 1)
-
     wanted = adp[...].astype(I32) - 1
     lane = iota((slots, LANES), 1) // rank
-    folded = jnp.zeros((slots, LANES), F32)
-    for n in range(homes // per):
-        folded += jnp.where(wanted == n * per + lane, got[:, n * LANES : (n + 1) * LANES], 0.0)
+
+    def fold(got):
+        total = jnp.zeros((slots, LANES), F32)
+        for n in range(homes // per):
+            total += jnp.where(wanted == n * per + lane, got[:, n * LANES : (n + 1) * LANES], 0.0)
+        return total
+
+    early[...] = fold(acc[...])
+    folded = early[...] + fold(shrink(CHUNKS - 1))
 
     low = jnp.sum(folded.T.reshape(per, rank, slots), axis=0)
     for i in range(NX):
@@ -580,6 +585,7 @@
             pltpu.VMEM((groups, tok), I32),
             pltpu.VMEM((2, groups, tok), I32),
             pltpu.VMEM((slots, LANES), F32),
+            pltpu.VMEM((slots, LANES), F32),
             pltpu.VMEM((NX, nz, BACK, LANES), F32),
             pltpu.VMEM((NX, rank, LANES), F32),
             pltpu.VMEM((peers // NEAR, NX, rank, LANES), F32),

time: 72.4 us -> 72.4 us (level)
  no operation moved by 1% of the time
where the time goes in v6:
time: 72.4 us; the launch traced here: 71.6 us
  Pallas kernels  69.8 us (96%)
  local copies, waits for them, and re-layouts  0.78 us (1%)
  between operations  0.76 us (1%)
    pallas_call x1, Pallas kernels, fused(): pl.pallas_call(functools.partial(fused_kernel, groups, peers), out_shape=...  69.8 us

profile of v6, /device:TPU:6, one launch (start us, length us, event | category | flops | bytes accessed | tf_op | source)
XLA Modules:
  0.0 71.6 jit_solution(7811979868983320143)
XLA Ops:
  0.0 0.0 copy-start
  0.0 0.0 copy-start.3
  0.0 0.0 copy-start.4
  0.0 0.0 copy-start.11
  0.0 69.8 %fused.1 = (bf16[32,24,64]{2,1,0:T(8,128)(2,1)S(1)}, s32[1,1]{1,0:T(1,128)}) custom-call(bf16[256,1024]{1,0:T(8,128)(2,1)} %x_hbm.1, bf16[1024,1024]{1,0:T(8,128)(2,1)} %v_hbm.1, bf16[512,1024]{1,0:T(8,128)(2,1)} %bitcast.77, bf16[512,64]{1,0:T(8,128)(2,1)} %bitcast.79, s32[64,128]{1,0:T(8,128)} %bitcast.80, s32[64,128]{1,0:T(8,128)} %bitcast.87, ...), custom_call_target="tpu_custom_call" | custom-call | tf_op jit(solution)/shard_map/fused/pallas_call | solution.py:558
  70.6 0.0 copy-done
  70.6 0.0 copy-done.3
  70.6 0.0 copy-done.4
  70.6 0.0 copy-done.11
  70.6 0.4 conditional.1
  70.6 0.1 copy.46
  71.0 0.0 copy-start.10
  71.0 0.6 copy-done.10
Async XLA Ops:
  0.0 70.6 %copy-start = (s32[1024]{0:T(1024)S(1)}, s32[1024]{0:T(1024)}, u32[]{:S(2)}) copy-start(s32[1024]{0:T(1024)} %param.17) | copy-start | bytes 12292
  0.0 70.6 %copy-start.3 = (bf16[32,16,64]{2,1,0:T(8,128)(2,1)S(1)}, bf16[32,16,64]{2,1,0:T(8,128)(2,1)}, u32[]{:S(2)}) copy-start(bf16[32,16,64]{2,1,0:T(8,128)(2,1)} %param.13) | copy-start | bytes 196612
  0.0 70.6 %copy-start.4 = (s32[8192]{0:T(1024)S(1)}, s32[8192]{0:T(1024)}, u32[]{:S(2)}) copy-start(s32[8192]{0:T(1024)} %param.14) | copy-start | bytes 98308
  0.0 70.6 %copy-start.11 = (s32[32,32]{1,0:T(8,128)S(1)}, s32[32,32]{1,0:T(8,128)}, u32[]{:S(2)}) copy-start(s32[32,32]{1,0:T(8,128)} %list_ref.1) | copy-start | bytes 12292
  71.0 0.6 copy-start.10
